TPU v7x, 128 devices: a whole 4x4x4 slice. The times are simulated.
128 devices in a mesh: stream: 8 (over y, core), girth: 16 (over z, x).
Axes of the slice: x: 4, y: 4, z: 4, core: 2. Of those that a mesh axis runs over, the one named last changes fastest.
Arguments:
- iterate: float32 [7, 16, 64, 256, 128], P(None, None, 'stream', 'girth'), may hold values from -6 to 6
- right_side: float32 [7, 16, 64, 256, 128], P(None, None, 'stream', 'girth'), may hold values from -6 to 6
- block_inverse: float32 [7, 7, 64, 256, 128], P(None, None, 'stream', 'girth'), may hold values from -0.6 to 1, as said below
- face_weight: float32 [6, 64, 256, 128], P(None, 'stream', 'girth'), may hold values from 0.05 to 0.5
- face_jacobian: float32 [6, 7, 7], replicated, may hold values from -2 to 2
- wall_cell: int32 [32768], P(('stream', 'girth')), may hold values from 0 to 16383
- wall_owner: int32 [32768, 1], P(('stream', 'girth')), may hold values from 0 to 127; in each aligned block of 256 rows (0 to 255, 256 to 511, ...) at most 8 rows name the same one
- wall_patch: int32 [32768], P(('stream', 'girth')), may hold values from 0 to 31
- wall_shape: float32 [32768, 8], P(('stream', 'girth')), may hold values from -20 to 20
Outputs:
- updated: float32 [7, 16, 64, 256, 128], P(None, None, 'stream', 'girth')
- patch_force: float32 [4096, 128], P(('stream', 'girth'))
- force: float32 [8, 16], replicated
Inputs may be any that keep to these rules, and one draw needn't show every extreme that they name: `block_inverse`: diagonal entries lie in 0.3 to 1, the others lie in -0.6 to 0.6. `wall_owner`: of the rows of one device at most 8 name one owner.
All inputs are finite; a program needn't handle non-finite values.
Results may differ from a plain program's by a relative error of at most 0.0001.
Values sent between devices are 32-bit elements; how exact they have to be, the bound alone decides.
A program may use at most 192 MiB of HBM per device.

v0:
```python
import jax
import jax.numpy as jnp
from jax import lax
from jax.sharding import PartitionSpec as P

PATCH_DEV = 32


def extended(block, sides, width):
    for axis, dim in sides:
        count = lax.axis_size(axis)
        forward = [(i, i + 1) for i in range(count - 1)]
        backward = [(target, source) for source, target in forward]
        low = lax.ppermute(
            lax.slice_in_dim(block, block.shape[dim] - width, None, axis=dim), axis, forward
        )
        high = lax.ppermute(lax.slice_in_dim(block, 0, width, axis=dim), axis, backward)
        block = jnp.concatenate([low, block, high], axis=dim)
    return block


def apply_jacobian(jacobian, field):
    return jnp.einsum("uv,vkxgr->ukxgr", jacobian, field, precision=lax.Precision.HIGHEST)


def shards(
    iterate,
    right_side,
    block_inverse,
    face_weight,
    face_jacobian,
    wall_cell,
    wall_owner,
    wall_patch,
    wall_shape,
):
    nvars, nrhs, cells_x, cells_g, cells_r = iterate.shape
    padded = extended(iterate, (("stream", 2), ("girth", 3)), 1)
    radial = jnp.pad(iterate, ((0, 0), (0, 0), (0, 0), (0, 0), (1, 1)))
    pieces = [
        padded[:, :, 0:cells_x, 1 : cells_g + 1],
        padded[:, :, 2 : cells_x + 2, 1 : cells_g + 1],
        padded[:, :, 1 : cells_x + 1, 0:cells_g],
        padded[:, :, 1 : cells_x + 1, 2 : cells_g + 2],
        radial[:, :, :, :, 0:cells_r],
        radial[:, :, :, :, 2 : cells_r + 2],
    ]
    images = [apply_jacobian(face_jacobian[face], pieces[face]) for face in range(6)]
    coupling = jnp.zeros(iterate.shape, jnp.float32)
    for face in range(6):
        coupling = coupling + face_weight[face][None, None] * images[face]
    remainder = right_side - coupling
    updated = jnp.zeros(iterate.shape, jnp.float32)
    for column in range(nvars):
        updated = updated + block_inverse[:, column][:, None] * remainder[column][None]
    wall_count = wall_cell.shape[0]
    modes = wall_shape.shape[1]
    pressure = updated[0].reshape(nrhs, cells_x * cells_g * cells_r)
    wall_values = jnp.transpose(jnp.take(pressure, wall_cell, axis=1))
    contribution = (wall_shape[:, :, None] * wall_values[:, None, :]).reshape(
        wall_count, modes * nrhs
    )
    stream_count = lax.axis_size("stream")
    girth_count = lax.axis_size("girth")
    devices = stream_count * girth_count
    capacity = 4 * wall_count // devices
    owner = wall_owner[:, 0]
    hits = (owner[:, None] == jnp.arange(devices, dtype=jnp.int32)[None, :]).astype(jnp.int32)
    before = jnp.cumsum(hits, axis=0) - hits
    placing = owner * capacity + jnp.sum(before * hits, axis=1)
    columns = contribution.shape[1]
    payload = jnp.zeros((devices * capacity, columns), jnp.float32).at[placing].set(contribution)
    labels = jnp.zeros((devices * capacity,), jnp.int32).at[placing].set(wall_patch)
    arrived, arrived_labels = (
        lax.all_to_all(payload, ("stream", "girth"), split_axis=0, concat_axis=0, tiled=True),
        lax.all_to_all(labels, ("stream", "girth"), split_axis=0, concat_axis=0, tiled=True),
    )
    member = (arrived_labels[:, None] == jnp.arange(PATCH_DEV, dtype=jnp.int32)[None, :]).astype(
        jnp.float32
    )
    patch_force = jnp.dot(
        jnp.transpose(member),
        arrived,
        precision=lax.Precision.HIGHEST,
        preferred_element_type=jnp.float32,
    )
    partial_sum = jnp.sum(patch_force, axis=0)
    total = lax.psum(partial_sum, ("stream", "girth"))
    force = (total / jnp.sqrt(jnp.float32(wall_count * devices))).reshape(modes, nrhs)
    return (updated, patch_force, force)


def solution(mesh):
    placed = (
        P(None, None, "stream", "girth", None),
        P(None, None, "stream", "girth", None),
        P(None, None, "stream", "girth", None),
        P(None, "stream", "girth", None),
        P(),
        P(("stream", "girth")),
        P(("stream", "girth"), None),
        P(("stream", "girth")),
        P(("stream", "girth"), None),
    )
    return jax.shard_map(
        shards,
        mesh=mesh,
        in_specs=placed,
        out_specs=(P(None, None, "stream", "girth", None), P(("stream", "girth"), None), P()),
        check_vma=False,
    )
```

profile of v0, /device:TPU:1, one launch (start us, length us, event | category | flops | bytes accessed | tf_op | source)
XLA Modules:
  0.0 267.8 jit_solution(12168604361553374628)
XLA Ops:
  0.6 3.0 %fusion.52 = (f32[7,16,1,16,128]{4,3,2,1,0:T(8,128)}, f32[7,16,1,16,128]{4,3,2,1,0:T(8,128)}) fusion(f32[7,16,8,16,128]{4,3,2,1,0:T(8,128)} %param.9), kind=kLoop, calls=%fused_computation.86 | loop fusion | bytes 3670016 | tf_op jit(solution)/shard_map/slice | solution.py:17
  3.7 4.6 %collective-permute-start = (f32[7,16,1,16,128]{4,3,2,1,0:T(8,128)}, f32[7,16,1,16,128]{4,3,2,1,0:T(8,128)}, u32[]{:S(2)}, u32[]{:S(2)}) collective-permute-start(f32[7,16,1,16,128]{4,3,2,1,0:T(8,128)} %get-tuple-element.13), channel_id=1, source_target_pairs={{0,16},{16,32},{32,48},{48,64},{64,80},{80,96},{96,112},{1,17},{17... | collective-permute-start | bytes 2752520 | tf_op jit(solution)/shard_map/ppermute | solution.py:14
  8.2 1.9 collective-permute-start.1
  10.2 0.8 copy.58
  11.3 0.9 fusion.27
  12.8 1.6 scatter_custom_fusion
  14.4 0.7 all_to_all.14
  15.1 10.9 %all-to-all-start = ((s32[128,8,1]{1,2,0:T(1,128)}), s32[128,8,1]{1,2,0:T(1,128)S(1)}, u32[]{:S(2)}, u32[]{:S(2)}) async-start(s32[128,8,1]{1,2,0:T(1,128)} %bitcast.46), calls=%async_computation | async-start | bytes 131072 | tf_op jit(solution)/shard_map/all_to_all | solution.py:76
  27.4 1.6 slice_bitcast_fusion.12
  29.1 3.7 %slice_bitcast_fusion.6 = (f32[7,8,16,128]{3,2,1,0:T(8,128)}, f32[7,8,16,128]{3,2,1,0:T(8,128)}, f32[7,8,16,128]{3,2,1,0:T(8,128)}, f32[7,8,16,128]{3,2,1,0:T(8,...) fusion(f32[7,7,8,16,128]{4,3,2,1,0:T(8,128)} %param.11), kind=kLoop, calls=%fused_computation.34 | loop fusion | bytes 6422528 | tf_op jit(solution)/shard_map/mul | solution.py:55
  32.8 3.1 %fusion.53 = (f32[7,16,1,16,128]{4,0,3,2,1:T(8,128)}, f32[7,16,10,16,128]{4,0,3,2,1:T(8,128)}) fusion(f32[7,16,1,16,128]{4,3,2,1,0:T(8,128)} %collective-permute-done), kind=kLoop, calls=%fused_computation.87 | loop fusion | bytes 3014656 | tf_op jit(solution)/shard_map/ppermute | solution.py:14
  35.9 11.6 %copy_dynamic-update-slice_fusion = (f32[7,16,10,16,128]{4,0,3,2,1:T(8,128)}, f32[7,16,8,16,128]{4,0,3,2,1:T(8,128)}) fusion(f32[7,16,10,16,128]{4,0,3,2,1:T(8,128)} %get-tuple-element.24, f32[7,16,8,16,128]{4,3,2,1,0:T(8,128)S(1)} %bitcast.107), kind=kLoop, calls=%fused_computation.55 | loop fusion | bytes 24117248
  47.5 12.6 %fusion.16 = f32[16,8,16,128,7]{3,4,2,1,0:T(8,128)S(1)} fusion(f32[7,16,8,16,128]{4,0,3,2,1:T(8,128)} %get-tuple-element.15, f32[6,7,7]{2,1,0:T(8,128)} %param.13), kind=kOutput, calls=%fused_computation.21 | convolution fusion | flops 154140672 | bytes 15732736 | tf_op jit(solution)/shard_map/uv,vkxgr->ukxgr/dot_general | solution.py:23
  60.2 11.4 %fusion.17 = f32[16,8,16,128,7]{3,4,2,1,0:T(8,128)} fusion(f32[7,16,8,16,128]{4,0,3,2,1:T(8,128)S(1)} %copy-done, f32[6,7,7]{2,1,0:T(8,128)} %param.13), kind=kOutput, calls=%fused_computation.22 | convolution fusion | flops 154140672 | bytes 14684160 | tf_op jit(solution)/shard_map/uv,vkxgr->ukxgr/dot_general | solution.py:23
  71.7 1.7 fusion.54
  73.7 3.3 %collective-permute-start.2 = (f32[7,16,10,1,128]{4,1,3,2,0:T(8,128)S(1)}, f32[7,16,10,1,128]{4,1,3,2,0:T(8,128)S(1)}, u32[]{:S(2)}, u32[]{:S(2)}) collective-permute-start(f32[7,16,10,1,128]{4,1,3,2,0:T(8,128)S(1)} %copy.52), channel_id=1, source_target_pairs={{0,1},{1,2},{2,3},{3,4},{4,5},{5,6},{6,7},{7,8},{8,9},{9,10},{10,1... | collective-permute-start | bytes 1720328 | tf_op jit(solution)/shard_map/ppermute | solution.py:14
  77.0 9.8 %fusion.12 = f32[16,8,16,128,7]{3,4,2,1,0:T(8,128)} fusion(f32[7,16,1,16,128]{4,0,3,2,1:T(8,128)S(1)} %get-tuple-element.25, f32[7,16,8,16,128]{4,0,3,2,1:T(8,128)S(1)} %copy-done, f32[6,7,7]{2,1,0:T(8,128)S(1)} %copy-done.11), kind=kOutput, calls=%fused_computation.17 | convolution fusion | flops 156205056 | bytes 16781312 | tf_op jit(solution)/shard_map/uv,vkxgr->ukxgr/dot_general | solution.py:23
  87.0 1.3 collective-permute-start.3
  88.3 9.9 %fusion.8 = f32[16,8,16,128,7]{3,4,2,1,0:T(8,128)} fusion(f32[7,16,8,16,128]{4,0,3,2,1:T(8,128)S(1)} %copy-done, f32[7,16,1,16,128]{4,0,3,2,1:T(8,128)S(1)} %copy-done.2, f32[6,7,7]{2,1,0:T(8,128)S(1)} %copy-done.11), kind=kOutput, calls=%fused_computation.13 | convolution fusion | flops 156205056 | bytes 16781312 | tf_op jit(solution)/shard_map/uv,vkxgr->ukxgr/dot_general | solution.py:23
  98.6 9.7 %fusion = f32[16,8,16,128,7]{3,4,2,1,0:T(8,128)} fusion(f32[7,16,10,16,128]{4,0,3,2,1:T(8,128)S(1)} %get-tuple-element.26, f32[7,16,10,1,128]{4,0,3,2,1:T(8,128)S(1)} %copy.53, f32[6,7,7]{2,1,0:T(8,128)S(1)} %copy-done.11), kind=kOutput, calls=%fused_computation.5 | convolution fusion | flops 156577792 | bytes 18485248 | tf_op jit(solution)/shard_map/uv,vkxgr->ukxgr/dot_general | solution.py:23
  108.6 23.7 %bitcast_subtract_fusion = f32[7,16,8,16,128]{4,0,3,2,1:T(8,128)} fusion(f32[7,16,8,16,128]{4,3,2,1,0:T(8,128)} %param.10, f32[16,8,16,128,7]{3,4,2,1,0:T(8,128)} %fusion.17, f32[16,8,16,128,7]{3,4,2,1,0:T(8,128)S(1)} %fusion.16, f32[16,8,16,128,7]{3,4,2,1,0:T(8,128)} %fusion, f32[16,8,16,128,7]{3,4,2,1,0:T(8,128)} %fusion.12, ...), kind=kOutput, calls=%fused_computation.23 | convolution fusion | flops 178597888 | bytes 63967232 | tf_op jit(solution)/shard_map/uv,vkxgr->ukxgr/dot_general | solution.py:23
  132.4 27.4 %fusion.51 = (f32[1,16,8,16,128]{4,0,3,2,1:T(1,128)S(1)}, f32[1,16,8,16,128]{4,0,3,2,1:T(1,128)S(1)}, f32[1,16,8,16,128]{4,0,3,2,1:T(1,128)S(1)}, f32[1,16,8,16,...) fusion(f32[7,16,8,16,128]{4,0,3,2,1:T(8,128)} %bitcast_subtract, ...), kind=kLoop, calls=%fused_computation.85 | loop fusion | bytes 14680064 | tf_op jit(solution)/shard_map/slice | solution.py:55
  159.9 3.9 %multiply_add_fusion = f32[7,16,8,16,128]{4,3,2,1,0:T(8,128)S(1)} fusion(f32[16,8,16,128]{3,2,1,0:T(8,128)S(1)} %bitcast.110, f32[7,8,16,128]{3,2,1,0:T(8,128)S(1)} %copy-done.8, f32[16,8,16,128]{3,2,1,0:T(8,128)S(1)} %bitcast.111, f32[7,8,16,128]{3,2,1,0:T(8,128)S(1)} %copy-done.9, f32[16,8,16,128]{3,2,1,0:T(8,128)S(1)} %bitcast.112, ...), kind=kLoop, calls=%fused_computation.24 | loop fusion | flops 23855104 | bytes 17891328 | tf_op jit(solution)/shard_map/add | solution.py:55
  163.8 3.0 %copy-done.1 = f32[7,16,8,16,128]{4,3,2,1,0:T(8,128)} copy-done((f32[7,16,8,16,128]{4,3,2,1,0:T(8,128)}, f32[7,16,8,16,128]{4,3,2,1,0:T(8,128)S(1)}, u32[]{:S(2)}) %copy-start.1) | copy-done | bytes 7340056
  166.9 4.6 %copy.61 = f32[1,16,8,16,128]{1,4,3,2,0:T(8,128)} copy(f32[1,16,8,16,128]{4,3,2,1,0:T(8,128)S(1)} %slice.172) | data formatting | bytes 2097152 | tf_op jit(solution)/shard_map/slice | solution.py:58
  171.6 4.1 %gather_fusion = f32[256,16]{1,0:T(8,128)S(1)} fusion(f32[16,16384]{0,1:T(8,128)} %bitcast.108, s32[1024]{0:T(1024)S(1)} %pad_clamp_fusion), kind=kCustom, calls=%fused_computation | custom fusion | bytes 33792 | tf_op jit(solution)/shard_map/jit(_take)/gather | solution.py:59
  176.0 1.9 scatter_custom_fusion.1
  177.9 11.0 %all-to-all-start.1 = ((f32[128,8,128]{2,1,0:T(8,128)}), f32[128,8,128]{2,1,0:T(8,128)S(1)}, u32[]{:S(2)}, u32[]{:S(2)}) async-start(f32[128,8,128]{2,1,0:T(8,128)} %bitcast.49), calls=%async_computation.1 | async-start | bytes 1048576 | tf_op jit(solution)/shard_map/all_to_all | solution.py:75
  189.4 0.8 reduce.3
  190.3 12.7 %all-to-all-done.1 = f32[128,8,128]{2,1,0:T(8,128)S(1)} async-done(((f32[128,8,128]{2,1,0:T(8,128)}), f32[128,8,128]{2,1,0:T(8,128)S(1)}, u32[]{:S(2)}, u32[]{:S(2)}) %all-to-all-start.1) | async-done | bytes 524320 | tf_op jit(solution)/shard_map/all_to_all | solution.py:75
  203.0 1.3 fusion.55
  204.4 62.5 %psum.7 = f32[128]{0:T(128)S(1)} all-reduce(f32[128]{0:T(128)S(1)} %get-tuple-element.33), channel_id=1, replica_groups=mesh['stream'=8,'girth'=16] {'stream','girth'}, use_global_device_ids=true, to_apply=%region_6.7 | all-reduce | flops 128 | bytes 1024 | tf_op jit(solution)/shard_map/psum | solution.py:88
  (67 shorter events, 5.2 us)
Async XLA Ops:
  0.6 35.3 %slice-start.3 = ((s8[7340032]{0:T(1024)(128)(4,1)}), s8[3145728]{0:T(1024)(128)(4,1)S(1)}, s32[]{:S(2)}) async-start(s8[7340032]{0:T(1024)(128)(4,1)} %bitcast.106), calls=%async_computation.5 | async-start | bytes 6291456
  3.7 29.2 %collective-permute-start = (f32[7,16,1,16,128]{4,3,2,1,0:T(8,128)}, f32[7,16,1,16,128]{4,3,2,1,0:T(8,128)}, u32[]{:S(2)}, u32[]{:S(2)}) collective-permute-start(f32[7,16,1,16,128]{4,3,2,1,0:T(8,128)} %get-tuple-element.13), channel_id=1, source_target_pairs={{0,16},{16,32},{32,48},{48,64},{64,80},{80,96},{96,112},{1,17},{17... | collective-permute-start | bytes 2752520 | tf_op jit(solution)/shard_map/ppermute | solution.py:14
  8.2 63.4 %collective-permute-start.1 = (f32[7,16,1,16,128]{4,3,2,1,0:T(8,128)}, f32[7,16,1,16,128]{4,3,2,1,0:T(8,128)}, u32[]{:S(2)}, u32[]{:S(2)}) collective-permute-start(f32[7,16,1,16,128]{4,3,2,1,0:T(8,128)} %get-tuple-element.12), channel_id=1, source_target_pairs={{16,0},{32,16},{48,32},{64,48},{80,64},{96,80},{112,96},{17,1},{33... | collective-permute-start | bytes 2752520 | tf_op jit(solution)/shard_map/ppermute | solution.py:17
  15.1 162.8 %all-to-all-start = ((s32[128,8,1]{1,2,0:T(1,128)}), s32[128,8,1]{1,2,0:T(1,128)S(1)}, u32[]{:S(2)}, u32[]{:S(2)}) async-start(s32[128,8,1]{1,2,0:T(1,128)} %bitcast.46), calls=%async_computation | async-start | bytes 131072 | tf_op jit(solution)/shard_map/all_to_all | solution.py:76
  29.1 6.8 %slice-start.4 = ((s8[7340032]{0:T(1024)(128)(4,1)}), s8[4194304]{0:T(1024)(128)(4,1)S(1)}, s32[]{:S(2)}) async-start(s8[7340032]{0:T(1024)(128)(4,1)} %bitcast.106), calls=%async_computation.6 | async-start | bytes 8388608
  47.5 12.6 %copy-start = (f32[7,16,8,16,128]{4,0,3,2,1:T(8,128)S(1)}, f32[7,16,8,16,128]{4,0,3,2,1:T(8,128)}, u32[]{:S(2)}) copy-start(f32[7,16,8,16,128]{4,0,3,2,1:T(8,128)} %get-tuple-element.15) | copy-start | bytes 22020100
  47.5 24.1 %slice-start = ((s8[10485760]{0:T(1024)(128)(4,1)}), s8[4194304]{0:T(1024)(128)(4,1)S(1)}, s32[]{:S(2)}) async-start(s8[10485760]{0:T(1024)(128)(4,1)} %bitcast.104), calls=%async_computation.2 | async-start | bytes 8388608
  47.5 24.1 %slice-start.1 = ((s8[10485760]{0:T(1024)(128)(4,1)}), s8[4194304]{0:T(1024)(128)(4,1)S(1)}, s32[]{:S(2)}) async-start(s8[10485760]{0:T(1024)(128)(4,1)} %bitcast.104), calls=%async_computation.3 | async-start | bytes 8388608
  60.2 11.5 %slice-start.2 = ((s8[10485760]{0:T(1024)(128)(4,1)}), s8[2097152]{0:T(1024)(128)(4,1)S(1)}, s32[]{:S(2)}) async-start(s8[10485760]{0:T(1024)(128)(4,1)} %bitcast.104), calls=%async_computation.4 | async-start | bytes 4194304
  60.2 16.8 %copy-start.11 = (f32[6,7,7]{2,1,0:T(8,128)S(1)}, f32[6,7,7]{2,1,0:T(8,128)}, u32[]{:S(2)}) copy-start(f32[6,7,7]{2,1,0:T(8,128)} %param.13) | copy-start | bytes 3532
  73.7 24.6 %collective-permute-start.2 = (f32[7,16,10,1,128]{4,1,3,2,0:T(8,128)S(1)}, f32[7,16,10,1,128]{4,1,3,2,0:T(8,128)S(1)}, u32[]{:S(2)}, u32[]{:S(2)}) collective-permute-start(f32[7,16,10,1,128]{4,1,3,2,0:T(8,128)S(1)} %copy.52), channel_id=1, source_target_pairs={{0,1},{1,2},{2,3},{3,4},{4,5},{5,6},{6,7},{7,8},{8,9},{9,10},{10,1... | collective-permute-start | bytes 1720328 | tf_op jit(solution)/shard_map/ppermute | solution.py:14
  77.0 11.3 %copy-start.2 = (f32[7,16,1,16,128]{4,0,3,2,1:T(8,128)S(1)}, f32[7,16,1,16,128]{4,0,3,2,1:T(8,128)}, u32[]{:S(2)}) copy-start(f32[7,16,1,16,128]{4,0,3,2,1:T(8,128)} %get-tuple-element.23) | copy-start | bytes 2752516
  87.0 21.3 %collective-permute-start.3 = (f32[7,16,10,1,128]{4,1,3,2,0:T(8,128)S(1)}, f32[7,16,10,1,128]{4,1,3,2,0:T(8,128)S(1)}, u32[]{:S(2)}, u32[]{:S(2)}) collective-permute-start(f32[7,16,10,1,128]{4,1,3,2,0:T(8,128)S(1)} %copy.54), channel_id=1, source_target_pairs={{1,0},{2,1},{3,2},{4,3},{5,4},{6,5},{7,6},{8,7},{9,8},{10,9},{11,1... | collective-permute-start | bytes 1720328 | tf_op jit(solution)/shard_map/ppermute | solution.py:17
  98.6 10.0 %copy-start.10 = (f32[8,16,128]{2,1,0:T(8,128)S(1)}, f32[8,16,128]{2,1,0:T(8,128)}, u32[]{:S(2)}) copy-start(f32[8,16,128]{2,1,0:T(8,128)} %get-tuple-element.32) | copy-start | bytes 196612
  132.4 27.5 %copy-start.3 = (f32[7,8,16,128]{3,2,1,0:T(8,128)S(1)}, f32[7,8,16,128]{3,2,1,0:T(8,128)}, u32[]{:S(2)}) copy-start(f32[7,8,16,128]{3,2,1,0:T(8,128)} %get-tuple-element.16) | copy-start | bytes 1376260
  132.4 27.5 %copy-start.4 = (f32[7,8,16,128]{3,2,1,0:T(8,128)S(1)}, f32[7,8,16,128]{3,2,1,0:T(8,128)}, u32[]{:S(2)}) copy-start(f32[7,8,16,128]{3,2,1,0:T(8,128)} %get-tuple-element.17) | copy-start | bytes 1376260
  132.4 27.5 %copy-start.5 = (f32[7,8,16,128]{3,2,1,0:T(8,128)S(1)}, f32[7,8,16,128]{3,2,1,0:T(8,128)}, u32[]{:S(2)}) copy-start(f32[7,8,16,128]{3,2,1,0:T(8,128)} %get-tuple-element.18) | copy-start | bytes 1376260
  132.4 27.5 %copy-start.6 = (f32[7,8,16,128]{3,2,1,0:T(8,128)S(1)}, f32[7,8,16,128]{3,2,1,0:T(8,128)}, u32[]{:S(2)}) copy-start(f32[7,8,16,128]{3,2,1,0:T(8,128)} %get-tuple-element.19) | copy-start | bytes 1376260
  132.4 27.5 %copy-start.7 = (f32[7,8,16,128]{3,2,1,0:T(8,128)S(1)}, f32[7,8,16,128]{3,2,1,0:T(8,128)}, u32[]{:S(2)}) copy-start(f32[7,8,16,128]{3,2,1,0:T(8,128)} %get-tuple-element.20) | copy-start | bytes 1376260
  132.4 27.5 %copy-start.8 = (f32[7,8,16,128]{3,2,1,0:T(8,128)S(1)}, f32[7,8,16,128]{3,2,1,0:T(8,128)}, u32[]{:S(2)}) copy-start(f32[7,8,16,128]{3,2,1,0:T(8,128)} %get-tuple-element.21) | copy-start | bytes 1376260
  132.4 27.5 %copy-start.9 = (f32[7,8,16,128]{3,2,1,0:T(8,128)S(1)}, f32[7,8,16,128]{3,2,1,0:T(8,128)}, u32[]{:S(2)}) copy-start(f32[7,8,16,128]{3,2,1,0:T(8,128)} %get-tuple-element.22) | copy-start | bytes 1376260
  163.8 3.1 %copy-start.1 = (f32[7,16,8,16,128]{4,3,2,1,0:T(8,128)}, f32[7,16,8,16,128]{4,3,2,1,0:T(8,128)S(1)}, u32[]{:S(2)}) copy-start(f32[7,16,8,16,128]{4,3,2,1,0:T(8,128)S(1)} %multiply_add_fusion) | copy-start | bytes 22020100
  166.8 9.0 %copy-start.12 = (f32[256,8]{0,1:T(8,128)S(1)}, f32[256,8]{0,1:T(8,128)}, u32[]{:S(2)}) copy-start(f32[256,8]{0,1:T(8,128)} %param.17) | copy-start | bytes 24580
  177.9 25.1 %all-to-all-start.1 = ((f32[128,8,128]{2,1,0:T(8,128)}), f32[128,8,128]{2,1,0:T(8,128)S(1)}, u32[]{:S(2)}, u32[]{:S(2)}) async-start(f32[128,8,128]{2,1,0:T(8,128)} %bitcast.49), calls=%async_computation.1 | async-start | bytes 1048576 | tf_op jit(solution)/shard_map/all_to_all | solution.py:75
where the time goes:
time: 271 us; the launch traced here: 268 us
  matrix products  78.5 us (29%)
  local copies, waits for them, and re-layouts  71.8 us (26%)
  blocking collectives  62.5 us (23%)
  starting transfers between devices  33.1 us (12%)
  waiting for transfers between devices  12.7 us (5%)
  other arithmetic  7.98 us (3%)
    dot_general x6, matrix products, apply_jacobian(): jnp.einsum('uv,vkxgr->ukxgr', jacobian, field, precision=lax.Precision.HI...  77.2 us
    psum x1, blocking collectives, shards(): total = lax.psum(partial_sum, ('stream', 'girth'))  62.5 us
    slice x1, local copies, waits for them, and re-layouts, shards(): remainder[column][None]  27.4 us
    unnamed x38, local copies, waits for them, and re-layouts  14.7 us
    all_to_all x1, waiting for transfers between devices, shards(): lax.all_to_all(payload, ('stream', 'girth'), split_axis=0, concat_axis=0,...  12.7 us
    all_to_all x1, starting transfers between devices, shards(): lax.all_to_all(payload, ('stream', 'girth'), split_axis=0, concat_axis=0,...  11 us
    all_to_all x1, starting transfers between devices, shards(): lax.all_to_all(labels, ('stream', 'girth'), split_axis=0, concat_axis=0,...  10.9 us
    ppermute x2, starting transfers between devices, extended(): lax.ppermute(lax.slice_in_dim(block, block.shape[dim] - width, None, axis...  7.91 us
  transfers between devices with their start and end apart: 6, of which 1 were waited for; matrix products, arithmetic and copies ran while one was open for 56% of the time, Pallas kernels for 0%

commit v1 on v0

v1 whole, which is shorter than its diff:
```python
import jax
import jax.numpy as jnp
from jax import lax
from jax.experimental import pallas as pl
from jax.experimental.pallas import tpu as pltpu
from jax.sharding import PartitionSpec as P

V = 7
K = 16
CX = 8
CG = 16
NR = 128
ROWS = CX * CG
SLOTS = 256
PATCH_DEV = 32
NS = 8
NG = 16
DEV = NS * NG
PAIRS = K // 2
PACK_1 = 2 * NG + 8
DEPTH = 176
BLK = V * 8
MESH = pl.DeviceIdType.MESH
HIGH = lax.Precision.HIGHEST
F32 = jnp.float32
BF16 = jnp.bfloat16
WEST, EAST, SOUTH, NORTH = range(4)


def nt(a, b, precision=None):
    return lax.dot_general(
        a, b, (((1,), (1,)), ((), ())), precision=precision, preferred_element_type=F32
    )


def split(x):
    hi = x.astype(BF16).astype(F32)
    return hi, x - hi


def operator(jacobian, turn):
    r = lax.broadcasted_iota(jnp.int32, (BLK, V), 0)
    c = lax.broadcasted_iota(jnp.int32, (BLK, V), 1)
    rows = (r // 8 == c).astype(F32)
    r = lax.broadcasted_iota(jnp.int32, (V, DEPTH), 0)
    c = lax.broadcasted_iota(jnp.int32, (V, DEPTH), 1)
    columns = ((c % BLK) // 8 == r).astype(F32)
    spread = jnp.dot(jnp.dot(rows, jacobian, precision=HIGH), columns, precision=HIGH)
    hi, lo = split(spread)
    r = lax.broadcasted_iota(jnp.int32, (BLK, DEPTH), 0)
    c = lax.broadcasted_iota(jnp.int32, (BLK, DEPTH), 1)
    keep = ((r + turn) % 8 == c % 8) & (c < 3 * BLK)
    return jnp.where(keep, jnp.where(c < 2 * BLK, hi, lo), 0.0)


def operand(load):
    x = jnp.concatenate([load(v) for v in range(V)], axis=0)
    hi, lo = split(x)
    pad = jnp.zeros((DEPTH - 3 * BLK, 2 * NR), F32)
    return jnp.concatenate([x, lo, x, pad], axis=0).astype(BF16)


def sweep_kernel(
    it, rhs, binv, fw, jac_in, cell_in, owner_in, patch_in, shape_in,
    upd, arrived_out,
    it_v, rhs_v, binv_v, fw_v, halo_x, halo_g, send_g, wmain, wside, edge, pick,
    jac, cell, owner, patch, shape, send_1, arrived_1, send_2, arrived_2,
    sem_it, sem_rhs, sem_misc, send_sem, recv_sem, send_sem_1, recv_sem_1, send_sem_2, recv_sem_2,
):
    s, g = lax.axis_index("stream"), lax.axis_index("girth")
    present = (s > 0, s < NS - 1, g > 0, g < NG - 1)
    target = ((s - 1, g), (s + 1, g), (s, g - 1), (s, g + 1))

    def it_copy(c):
        ks = pl.ds(2 * c, 2)
        return pltpu.make_async_copy(it.at[:, ks], it_v.at[:, ks], sem_it.at[c])

    def rhs_copy(c):
        ks = pl.ds(2 * c, 2)
        return pltpu.make_async_copy(rhs.at[:, ks], rhs_v.at[:, ks], sem_rhs.at[c])

    singles = [
        pltpu.make_async_copy(a, b, sem_misc.at[i])
        for i, (a, b) in enumerate(
            (
                (jac_in, jac),
                (cell_in, cell),
                (owner_in, owner),
                (patch_in, patch),
                (shape_in, shape),
                (fw, fw_v),
                (binv, binv_v),
            )
        )
    ]

    def halo_copy(side, c, land=None):
        land = side ^ 1 if land is None else land
        ks = pl.ds(2 * c, 2)
        if side in (WEST, EAST):
            rows = pl.ds(0 if side == WEST else ROWS - CG, CG)
            src, dst = it.at[:, ks, rows], halo_x.at[land, :, ks]
        else:
            src, dst = send_g.at[side - 2, :, ks], halo_g.at[land - 2, :, ks]
        return pltpu.make_async_remote_copy(
            src_ref=src,
            dst_ref=dst,
            send_sem=send_sem.at[side, c],
            recv_sem=recv_sem.at[land, c],
            device_id=target[side],
            device_id_type=MESH,
        )

    def stream_copy(step, land):
        to = lax.rem(s + step, NS)
        return pltpu.make_async_remote_copy(
            src_ref=send_1.at[to],
            dst_ref=arrived_1.at[pl.ds(land * PACK_1, PACK_1)],
            send_sem=send_sem_1.at[step],
            recv_sem=recv_sem_1.at[land],
            device_id=(to, g),
            device_id_type=MESH,
        )

    def girth_copy(step, land):
        to = lax.rem(g + step, NG)
        return pltpu.make_async_remote_copy(
            src_ref=send_2.at[to],
            dst_ref=arrived_2.at[land],
            send_sem=send_sem_2.at[step],
            recv_sem=recv_sem_2.at[land],
            device_id=(s, to),
            device_id_type=MESH,
        )

    for copy in singles[:5]:
        copy.start()
    for c in range(PAIRS):
        it_copy(c).start()
    for copy in singles[5:]:
        copy.start()
    for c in range(PAIRS):
        rhs_copy(c).start()

    barrier = pltpu.get_barrier_semaphore()
    for step in range(1, NS):
        pl.semaphore_signal(
            barrier, inc=1, device_id=(lax.rem(s + step, NS), g), device_id_type=MESH
        )
    for step in range(1, NG):
        pl.semaphore_signal(
            barrier, inc=1, device_id=(s, lax.rem(g + step, NG)), device_id_type=MESH
        )

    for side in range(4):

        @pl.when(jnp.logical_not(present[side]))
        def _():
            if side in (WEST, EAST):
                halo_x[side] = jnp.zeros((V, K, CG, NR), F32)
            else:
                halo_g[side - 2] = jnp.zeros((V, K, CX, NR), F32)

    for copy in singles[:5]:
        copy.wait()

    turns = (0, 0, 7, 1, 0, 0)
    wmain[...] = jnp.concatenate(
        [operator(jac[f], turns[f]) for f in range(6)], axis=0
    ).astype(BF16)
    pad = jnp.zeros((64 - BLK, DEPTH), F32)
    for f in range(4):
        wside[f] = jnp.concatenate([operator(jac[f], 0), pad], axis=0).astype(BF16)

    pl.semaphore_wait(barrier, NS + NG - 2)

    for c in range(PAIRS):
        for side in (WEST, EAST):

            @pl.when(present[side])
            def _():
                halo_copy(side, c).start()

    for c in range(PAIRS):
        it_copy(c).wait()
        for k in (2 * c, 2 * c + 1):
            for v in range(V):
                send_g[0, v, k] = it_v[v, k, pl.ds(0, CX, stride=CG), :]
                send_g[1, v, k] = it_v[v, k, pl.ds(CG - 1, CX, stride=CG), :]

        for side in (SOUTH, NORTH):

            @pl.when(present[side])
            def _():
                halo_copy(side, c).start()

    names = (owner[...] == lax.broadcasted_iota(jnp.int32, (DEV, SLOTS), 0)).astype(F32)
    r = lax.broadcasted_iota(jnp.int32, (SLOTS, SLOTS), 0)
    c = lax.broadcasted_iota(jnp.int32, (SLOTS, SLOTS), 1)
    earlier = jnp.dot(names.astype(BF16), (r < c).astype(BF16), preferred_element_type=F32)
    place = jnp.sum(names * earlier, axis=0, keepdims=True).astype(jnp.int32)

    for copy in singles[5:]:
        copy.wait()

    sub = lax.broadcasted_iota(jnp.int32, (8, NR), 0)
    lane = lax.broadcasted_iota(jnp.int32, (8, NR), 1)

    def main(c):
        k0 = 2 * c

        def rows(x, t):
            return pl.ds(x * CG + 8 * t, 8)

        def pair(ref, *at):
            return jnp.concatenate([ref[at[0], k0 + j, *at[1:]] for j in range(2)], axis=1)

        def finish(x, left, image):
            for t in range(2):
                w = fw_v[1, rows(x, t), :]
                rem = [
                    [left[t][j][u] - w * image[t][u * 8 : u * 8 + 8, j * NR : (j + 1) * NR] for u in range(V)]
                    for j in range(2)
                ]
                for u in range(V):
                    acc = [None, None]
                    for v in range(V):
                        b = binv_v[u, v, rows(x, t), :]
                        for j in range(2):
                            term = b * rem[j][v]
                            acc[j] = term if acc[j] is None else acc[j] + term
                    for j in range(2):
                        upd[u, k0 + j, rows(x, t), :] = acc[j]

        def outer(side, t):
            return jnp.dot(
                wside[side],
                operand(lambda v: pair(halo_x.at[side], v, pl.ds(8 * t, 8))),
                preferred_element_type=F32,
            )

        for side in range(2):
            edge[side] = jnp.dot(
                wside[2 + side],
                operand(lambda v: pair(halo_g.at[side], v)),
                preferred_element_type=F32,
            )
        before, left_before = [outer(WEST, t) for t in range(2)], None
        for x in range(CX):
            y = [
                jnp.dot(
                    wmain[...],
                    operand(lambda v, t=t: pair(it_v, v, rows(x, t))),
                    preferred_element_type=F32,
                )
                for t in range(2)
            ]

            def part(t, f, u, j):
                at = f * BLK + u * 8
                return y[t][at : at + 8, j * NR : (j + 1) * NR]

            w = [[fw_v[f, rows(x, t), :] for f in range(6)] for t in range(2)]
            for t in range(2):
                w[t][4] = jnp.where(lane == 0, 0.0, w[t][4])
                w[t][5] = jnp.where(lane == NR - 1, 0.0, w[t][5])
            left = [[[None] * V for _ in range(2)] for _ in range(2)]
            for t in range(2):
                for j in range(2):
                    for u in range(V):
                        at = u * 8 + x
                        if t == 0:
                            first = edge[0, at : at + 1, j * NR : (j + 1) * NR]
                            last = part(1, 3, u, j)
                        else:
                            first = part(0, 2, u, j)
                            last = edge[1, at : at + 1, j * NR : (j + 1) * NR]
                        y2 = jnp.where(sub == 0, first, part(t, 2, u, j))
                        y3 = jnp.where(sub == 7, last, part(t, 3, u, j))
                        total = w[t][2] * y2 + w[t][3] * y3
                        total += w[t][4] * pltpu.roll(part(t, 4, u, j), 1, axis=1)
                        total += w[t][5] * pltpu.roll(part(t, 5, u, j), NR - 1, axis=1)
                        total += w[t][0] * before[t][u * 8 : u * 8 + 8, j * NR : (j + 1) * NR]
                        left[t][j][u] = rhs_v[u, k0 + j, rows(x, t), :] - total
            if x > 0:
                finish(x - 1, left_before, [y[t][BLK : 2 * BLK] for t in range(2)])
            before, left_before = [y[t][0:BLK] for t in range(2)], left
        finish(CX - 1, left_before, [outer(EAST, t) for t in range(2)])

    r = lax.broadcasted_iota(jnp.int32, (2 * NR, SLOTS), 0)
    lanes = (cell[...] % NR == r % NR).astype(BF16)
    r = lax.broadcasted_iota(jnp.int32, (ROWS, SLOTS), 0)
    on_row = (cell[...] // NR == r).astype(F32)

    @pl.loop(0, PAIRS)
    def _(c):
        rhs_copy(c).wait()
        for side in range(4):

            @pl.when(present[side])
            def _():
                halo_copy(side, c, side).wait_recv()

        main(c)
        for j in range(2):
            hi, lo = split(upd[0, 2 * c + j])
            both = jnp.concatenate([hi, lo], axis=1).astype(BF16)
            found = jnp.dot(both, lanes, preferred_element_type=F32) * on_row
            pick[pl.ds(2 * c + j, 1), :] = jnp.sum(found, axis=0, keepdims=True)

    pressure = pick[...]
    shapes = shape[...]
    values = jnp.concatenate(
        [pressure, shapes, jnp.broadcast_to(patch[...].astype(F32), (8, SLOTS))], axis=0
    )
    spread = jnp.concatenate([values] * 4, axis=0)
    group = lax.broadcasted_iota(jnp.int32, (NR, SLOTS), 0) // 32
    chosen = names.astype(BF16)
    chosen = jnp.concatenate([chosen, chosen], axis=1)
    for half in range(2):
        hi, lo = split(jnp.where(place == 4 * half + group, spread, 0.0))
        packed = nt(chosen, jnp.concatenate([hi, lo], axis=1).astype(BF16))
        send_1[:, NG * half : NG * (half + 1), :] = packed.reshape(NS, NG, NR)
    products = jnp.concatenate([shapes[m : m + 1] * pressure for m in range(8)], axis=0)
    sums = nt(jnp.ones((8, SLOTS), F32), products, HIGH)
    send_1[:, 2 * NG :, :] = jnp.broadcast_to(sums[None], (NS, 8, NR))

    for step in range(1, NS):
        stream_copy(step, s).start()
    arrived_1[pl.ds(pl.multiple_of(s * PACK_1, 8), PACK_1), :] = send_1[s]
    for step in range(1, NS):
        stream_copy(step, lax.rem(s + NS - step, NS)).wait_recv()
    for to in range(NG):
        for half in range(2):
            send_2[to, 8 * half : 8 * half + 8, :] = arrived_1[
                pl.ds(half * NG + to, NS, stride=PACK_1), :
            ]
    sums = jnp.sum(arrived_1[pl.ds(2 * NG, NS, stride=PACK_1), :], axis=0, keepdims=True)
    send_2[:, 16:, :] = jnp.broadcast_to(sums[None], (NG, 8, NR))
    for step in range(1, NG):
        girth_copy(step, g).start()
    arrived_2[g] = send_2[g]
    for step in range(1, NG):
        girth_copy(step, lax.rem(g + NG - step, NG)).wait_recv()
    arrived_out[...] = arrived_2[...]

    for c in range(PAIRS):
        for side in range(4):

            @pl.when(present[side])
            def _():
                halo_copy(side, c).wait_send()

    for step in range(1, NS):
        stream_copy(step, s).wait_send()
    for step in range(1, NG):
        girth_copy(step, g).wait_send()


def force_kernel(upd, arrived, upd_out, patch_out, force_out, patch_force, force, sem):
    copies = [
        pltpu.make_async_copy(upd.at[v], upd_out.at[v], sem.at[v]) for v in range(V)
    ]
    for copy in copies:
        copy.start()

    lane = lax.broadcasted_iota(jnp.int32, (2 * NR, NR), 0) % NR
    column = lax.broadcasted_iota(jnp.int32, (2 * NR, NR), 1)
    patch = lax.broadcasted_iota(jnp.int32, (DEV, NR), 1).astype(F32)
    total = None
    for half in range(2):
        hi, lo = split(arrived[:, 8 * half : 8 * half + 8, :].reshape(DEV, NR))
        both = jnp.concatenate([hi, lo], axis=1).astype(BF16)
        for j in range(4):
            base = 32 * j
            by_shape = (lane == base + K + column // K).astype(BF16)
            by_rhs = (lane == base + column % K).astype(BF16)
            by_patch = (lane == base + 24).astype(BF16)
            contribution = jnp.dot(both, by_shape, preferred_element_type=F32) * jnp.dot(
                both, by_rhs, preferred_element_type=F32
            )
            label = jnp.dot(both, by_patch, preferred_element_type=F32)
            member = (label == patch).astype(F32).T[0:PATCH_DEV].astype(BF16)
            hi, lo = split(contribution)
            term = jnp.dot(member, hi.astype(BF16), preferred_element_type=F32) + jnp.dot(
                member, lo.astype(BF16), preferred_element_type=F32
            )
            total = term if total is None else total + term
    patch_force[...] = total
    out_patch = pltpu.make_async_copy(patch_force, patch_out, sem.at[V])
    out_patch.start()
    sums = jnp.sum(arrived[:, 16, :], axis=0, keepdims=True) / jnp.sqrt(F32(DEV * SLOTS))
    r = lax.broadcasted_iota(jnp.int32, (8, NR), 0)
    c = lax.broadcasted_iota(jnp.int32, (8, NR), 1)
    rows = jnp.where(c // K == r, sums, 0.0)
    r = lax.broadcasted_iota(jnp.int32, (K, NR), 0)
    c = lax.broadcasted_iota(jnp.int32, (K, NR), 1)
    force[...] = nt(rows, (c % K == r).astype(F32), HIGH)
    out_force = pltpu.make_async_copy(force, force_out, sem.at[V + 1])
    out_force.start()
    for copy in copies:
        copy.wait()
    out_patch.wait()
    out_force.wait()


def shards(iterate, right_side, block_inverse, face_weight, face_jacobian, wall_cell, wall_owner, wall_patch, wall_shape):
    hbm = pl.BlockSpec(memory_space=pltpu.HBM)
    vmem = pl.BlockSpec(memory_space=pltpu.VMEM)
    dma = pltpu.SemaphoreType.DMA
    operands = (
        iterate.reshape(V, K, ROWS, NR),
        right_side.reshape(V, K, ROWS, NR),
        block_inverse.reshape(V, V, ROWS, NR),
        face_weight.reshape(6, ROWS, NR),
        face_jacobian,
        wall_cell.reshape(1, SLOTS),
        wall_owner.reshape(1, SLOTS),
        wall_patch.reshape(1, SLOTS),
        wall_shape.T,
    )
    updated, arrived = pl.pallas_call(
        sweep_kernel,
        out_shape=(
            pltpu.VMEM((V, K, ROWS, NR), F32),
            pltpu.VMEM((NG, 24, NR), F32),
        ),
        in_specs=[hbm] * 9,
        out_specs=(vmem, vmem),
        scratch_shapes=[
            pltpu.VMEM((V, K, ROWS, NR), F32),
            pltpu.VMEM((V, K, ROWS, NR), F32),
            pltpu.VMEM((V, V, ROWS, NR), F32),
            pltpu.VMEM((6, ROWS, NR), F32),
            pltpu.VMEM((2, V, K, CG, NR), F32),
            pltpu.VMEM((2, V, K, CX, NR), F32),
            pltpu.VMEM((2, V, K, CX, NR), F32),
            pltpu.VMEM((6 * BLK, DEPTH), BF16),
            pltpu.VMEM((4, 64, DEPTH), BF16),
            pltpu.VMEM((2, 64, 2 * NR), F32),
            pltpu.VMEM((K, SLOTS), F32),
            pltpu.VMEM((6, V, V), F32),
            pltpu.VMEM((1, SLOTS), jnp.int32),
            pltpu.VMEM((1, SLOTS), jnp.int32),
            pltpu.VMEM((1, SLOTS), jnp.int32),
            pltpu.VMEM((8, SLOTS), F32),
            pltpu.VMEM((NS, PACK_1, NR), F32),
            pltpu.VMEM((NS * PACK_1, NR), F32),
            pltpu.VMEM((NG, 24, NR), F32),
            pltpu.VMEM((NG, 24, NR), F32),
            dma((PAIRS,)),
            dma((PAIRS,)),
            dma((7,)),
            dma((4, PAIRS)),
            dma((4, PAIRS)),
            dma((NS,)),
            dma((NS,)),
            dma((NG,)),
            dma((NG,)),
        ],
        compiler_params=pltpu.CompilerParams(
            collective_id=0, has_side_effects=True, vmem_limit_bytes=32 * 1024 * 1024
        ),
    )(*[pltpu.with_memory_space_constraint(x, pltpu.HBM) for x in operands])
    updated, patch_force, force = pl.pallas_call(
        force_kernel,
        out_shape=(
            pltpu.HBM((V, K, ROWS, NR), F32),
            pltpu.HBM((PATCH_DEV, NR), F32),
            pltpu.HBM((8, K), F32),
        ),
        in_specs=[vmem, vmem],
        out_specs=(hbm, hbm, hbm),
        scratch_shapes=[
            pltpu.VMEM((PATCH_DEV, NR), F32),
            pltpu.VMEM((8, K), F32),
            dma((V + 2,)),
        ],
        compiler_params=pltpu.CompilerParams(vmem_limit_bytes=8 * 1024 * 1024),
    )(
        pltpu.with_memory_space_constraint(updated, pltpu.VMEM),
        pltpu.with_memory_space_constraint(arrived, pltpu.VMEM),
    )
    return (updated.reshape(V, K, CX, CG, NR), patch_force, force)


def solution(mesh):
    placed = (
        P(None, None, "stream", "girth", None),
        P(None, None, "stream", "girth", None),
        P(None, None, "stream", "girth", None),
        P(None, "stream", "girth", None),
        P(),
        P(("stream", "girth")),
        P(("stream", "girth"), None),
        P(("stream", "girth")),
        P(("stream", "girth"), None),
    )
    return jax.shard_map(
        shards,
        mesh=mesh,
        in_specs=placed,
        out_specs=(P(None, None, "stream", "girth", None), P(("stream", "girth"), None), P()),
        check_vma=False,
    )
```

time: 271 us -> 44.3 us (0.16); the launches traced: 268 us -> 44.1 us
  matrix products: 78.5 us -> 0 us
  local copies, waits for them, and re-layouts: 71.8 us -> 0 us
  blocking collectives: 62.5 us -> 0 us
  Pallas kernels: 0 us -> 43.4 us
  starting transfers between devices: 33.1 us -> 0 us
  waiting for transfers between devices: 12.7 us -> 0 us
  other arithmetic: 7.98 us -> 0 us
    dot_general x7 -> x0, matrix products: 78.5 us -> none  [the longest x6 77.2 us: apply_jacobian(): jnp.einsum('uv,vkxgr->ukxgr', jacobian, field, precision=lax.Precision.HI...]
    psum x1 -> x0, blocking collectives: 62.5 us -> none  [shards(): total = lax.psum(partial_sum, ('stream', 'girth'))]
    pallas_call x0 -> x2, Pallas kernels: none -> 43.4 us  [the longest x1 40.3 us: shards(): pl.pallas_call(sweep_kernel, out_shape=(pltpu.VMEM((V, K, ROWS, NR), F32)...]
    slice x7 -> x0, local copies, waits for them, and re-layouts: 35.6 us -> none  [the longest x1 27.4 us: shards(): remainder[column][None]]
    all_to_all x2 -> x0, starting transfers between devices: 21.9 us -> none  [the longest x1 11 us: shards(): lax.all_to_all(payload, ('stream', 'girth'), split_axis=0, concat_axis=0,...]
    unnamed x38 -> x0, local copies, waits for them, and re-layouts: 14.7 us -> none
    all_to_all x2 -> x0, waiting for transfers between devices: 12.7 us -> none  [the longest x1 12.7 us: shards(): lax.all_to_all(payload, ('stream', 'girth'), split_axis=0, concat_axis=0,...]
    ppermute x4 -> x0, starting transfers between devices: 11.1 us -> none  [the longest x2 7.91 us: extended(): lax.ppermute(lax.slice_in_dim(block, block.shape[dim] - width, None, axis...]
  transfers between devices with their start and end apart: 6 -> 0, of which waited for: 1 -> 0; matrix products, arithmetic and copies ran while one was open for 56% -> 0% of each run, Pallas kernels for 0% -> 0%
where the time goes in v1:
time: 44.3 us; the launch traced here: 44.1 us
  Pallas kernels  43.4 us (98%)
  between operations  0.64 us (1%)
    pallas_call x1, Pallas kernels, shards(): pl.pallas_call(sweep_kernel, out_shape=(pltpu.VMEM((V, K, ROWS, NR), F32)...  40.3 us
    pallas_call x1, Pallas kernels, shards(): pl.pallas_call(force_kernel, out_shape=(pltpu.HBM((V, K, ROWS, NR), F32),...  3.07 us

profile of v1, /device:TPU:1, one launch (start us, length us, event | category | flops | bytes accessed | tf_op | source)
XLA Modules:
  0.0 44.1 jit_solution(4328091685916865692)
XLA Ops:
  0.6 40.3 %shard_map.112 = (f32[7,16,128,128]{3,2,1,0:T(8,128)S(1)}, f32[16,24,128]{2,1,0:T(8,128)S(1)}) custom-call(f32[7,16,128,128]{3,2,1,0:T(8,128)} %bitcast.9, f32[7,16,128,128]{3,2,1,0:T(8,128)} %bitcast.10, f32[7,7,128,128]{3,2,1,0:T(8,128)} %bitcast.11, f32[6,128,128]{2,1,0:T(8,128)} %bitcast.12, f32[6,7,7]{2,1,0:T(8,128)} %jac_in.1, s32[1,256]{1,0:T(1,128)} %bitcast.14, ...), custom_call_target="tpu_custom_call" | custom-call | tf_op jit(solution)/shard_map/pallas_call | solution.py:422
  41.0 3.1 %shard_map.113 = (f32[7,16,128,128]{3,2,1,0:T(8,128)}, f32[32,128]{1,0:T(8,128)}, f32[8,16]{1,0:T(8,128)}) custom-call(f32[7,16,128,128]{3,2,1,0:T(8,128)S(1)} %get-tuple-element.8.upd, f32[16,24,128]{2,1,0:T(8,128)S(1)} %get-tuple-element.9.arrived), custom_call_target="tpu_custom_call" | custom-call | tf_op jit(solution)/shard_map/pallas_call | solution.py:465

commit v2 on v1

--- a/solution.py
+++ b/solution.py
@@ -18,8 +18,10 @@
 DEV = NS * NG
 PAIRS = K // 2
 PACK_1 = 2 * NG + 8
-DEPTH = 176
+REST_1 = 32
 BLK = V * 8
+TERM = 64
+DEPTH = 3 * TERM
 MESH = pl.DeviceIdType.MESH
 HIGH = lax.Precision.HIGHEST
 F32 = jnp.float32
@@ -44,28 +46,29 @@
     rows = (r // 8 == c).astype(F32)
     r = lax.broadcasted_iota(jnp.int32, (V, DEPTH), 0)
     c = lax.broadcasted_iota(jnp.int32, (V, DEPTH), 1)
-    columns = ((c % BLK) // 8 == r).astype(F32)
+    columns = ((c % TERM) // 8 == r).astype(F32)
     spread = jnp.dot(jnp.dot(rows, jacobian, precision=HIGH), columns, precision=HIGH)
     hi, lo = split(spread)
     r = lax.broadcasted_iota(jnp.int32, (BLK, DEPTH), 0)
     c = lax.broadcasted_iota(jnp.int32, (BLK, DEPTH), 1)
-    keep = ((r + turn) % 8 == c % 8) & (c < 3 * BLK)
-    return jnp.where(keep, jnp.where(c < 2 * BLK, hi, lo), 0.0)
+    keep = (r + turn) % 8 == c % 8
+    return jnp.where(keep, jnp.where(c < 2 * TERM, hi, lo), 0.0)
 
 
 def operand(load):
-    x = jnp.concatenate([load(v) for v in range(V)], axis=0)
-    hi, lo = split(x)
-    pad = jnp.zeros((DEPTH - 3 * BLK, 2 * NR), F32)
-    return jnp.concatenate([x, lo, x, pad], axis=0).astype(BF16)
+    pad = jnp.zeros((TERM - BLK, 2 * NR), F32)
+    x = jnp.concatenate([load(v) for v in range(V)] + [pad], axis=0)
+    hi = x.astype(BF16)
+    lo = (x - hi.astype(F32)).astype(BF16)
+    return jnp.concatenate([hi, lo, hi], axis=0)
 
 
 def sweep_kernel(
     it, rhs, binv, fw, jac_in, cell_in, owner_in, patch_in, shape_in,
     upd, arrived_out,
-    it_v, rhs_v, binv_v, fw_v, halo_x, halo_g, send_g, wmain, wside, edge, pick,
+    it_v, rhs_v, binv_v, fw_v, halo_x, halo_g, send_g, wmain, wside, pick,
     jac, cell, owner, patch, shape, send_1, arrived_1, send_2, arrived_2,
-    sem_it, sem_rhs, sem_misc, send_sem, recv_sem, send_sem_1, recv_sem_1, send_sem_2, recv_sem_2,
+    sem_it, sem_rhs, sem_misc, send_sem, recv_sem, send_sem_1, recv_sem_1, send_sem_2, recv_sem_2, relay,
 ):
     s, g = lax.axis_index("stream"), lax.axis_index("girth")
     present = (s > 0, s < NS - 1, g > 0, g < NG - 1)
@@ -99,7 +102,7 @@
         ks = pl.ds(2 * c, 2)
         if side in (WEST, EAST):
             rows = pl.ds(0 if side == WEST else ROWS - CG, CG)
-            src, dst = it.at[:, ks, rows], halo_x.at[land, :, ks]
+            src, dst = it_v.at[:, ks, rows], halo_x.at[land, :, ks]
         else:
             src, dst = send_g.at[side - 2, :, ks], halo_g.at[land - 2, :, ks]
         return pltpu.make_async_remote_copy(
@@ -133,6 +136,29 @@
             device_id_type=MESH,
         )
 
+    def ring(axis, step):
+        if axis == 0:
+            return (lax.rem(s + step + NS, NS), g)
+        return (s, lax.rem(g + step + NG, NG))
+
+    def relay_signal(axis, level):
+        for way in range(2):
+            pl.semaphore_signal(
+                relay.at[axis, level, way],
+                inc=1,
+                device_id=ring(axis, (1 << level) * (1 - 2 * way)),
+                device_id_type=MESH,
+            )
+
+    def relay_wait(axis, level):
+        for way in range(2):
+            pl.semaphore_wait(relay.at[axis, level, way], 1)
+
+    barrier = pltpu.get_barrier_semaphore()
+    for axis in range(2):
+        for step in (1, -1):
+            pl.semaphore_signal(barrier, inc=1, device_id=ring(axis, step), device_id_type=MESH)
+
     for copy in singles[:5]:
         copy.start()
     for c in range(PAIRS):
@@ -142,16 +168,6 @@
     for c in range(PAIRS):
         rhs_copy(c).start()
 
-    barrier = pltpu.get_barrier_semaphore()
-    for step in range(1, NS):
-        pl.semaphore_signal(
-            barrier, inc=1, device_id=(lax.rem(s + step, NS), g), device_id_type=MESH
-        )
-    for step in range(1, NG):
-        pl.semaphore_signal(
-            barrier, inc=1, device_id=(s, lax.rem(g + step, NG)), device_id_type=MESH
-        )
-
     for side in range(4):
 
         @pl.when(jnp.logical_not(present[side]))
@@ -165,21 +181,13 @@
         copy.wait()
 
     turns = (0, 0, 7, 1, 0, 0)
+    parts = [operator(jac[f], turns[f]) for f in range(6)]
     wmain[...] = jnp.concatenate(
-        [operator(jac[f], turns[f]) for f in range(6)], axis=0
+        [parts[f][8 * u : 8 * u + 8] for u in range(V) for f in range(6)], axis=0
     ).astype(BF16)
-    pad = jnp.zeros((64 - BLK, DEPTH), F32)
+    pad = jnp.zeros((TERM - BLK, DEPTH), F32)
     for f in range(4):
         wside[f] = jnp.concatenate([operator(jac[f], 0), pad], axis=0).astype(BF16)
-
-    pl.semaphore_wait(barrier, NS + NG - 2)
-
-    for c in range(PAIRS):
-        for side in (WEST, EAST):
-
-            @pl.when(present[side])
-            def _():
-                halo_copy(side, c).start()
 
     for c in range(PAIRS):
         it_copy(c).wait()
@@ -188,11 +196,17 @@
                 send_g[0, v, k] = it_v[v, k, pl.ds(0, CX, stride=CG), :]
                 send_g[1, v, k] = it_v[v, k, pl.ds(CG - 1, CX, stride=CG), :]
 
-        for side in (SOUTH, NORTH):
+    pl.semaphore_wait(barrier, 4)
+
+    for c in range(PAIRS):
+        for side in range(4):
 
             @pl.when(present[side])
             def _():
                 halo_copy(side, c).start()
+
+    relay_signal(0, 0)
+    relay_signal(1, 0)
 
     names = (owner[...] == lax.broadcasted_iota(jnp.int32, (DEV, SLOTS), 0)).astype(F32)
     r = lax.broadcasted_iota(jnp.int32, (SLOTS, SLOTS), 0)
@@ -206,86 +220,110 @@
     sub = lax.broadcasted_iota(jnp.int32, (8, NR), 0)
     lane = lax.broadcasted_iota(jnp.int32, (8, NR), 1)
 
+    def rows(x, t):
+        return pl.ds(x * CG + 8 * t, 8)
+
+    def borders(c):
+        k0 = 2 * c
+        for side in range(4):
+            for t in range(2 if side in (WEST, EAST) else 1):
+                if side in (WEST, EAST):
+                    at = rows(0 if side == WEST else CX - 1, t)
+
+                    def load(v):
+                        return jnp.concatenate(
+                            [halo_x[side, v, k0 + j, pl.ds(8 * t, 8), :] for j in range(2)], axis=1
+                        )
+                else:
+                    at = pl.ds(0 if side == SOUTH else CG - 1, CX, stride=CG)
+
+                    def load(v):
+                        return jnp.concatenate([halo_g[side - 2, v, k0 + j] for j in range(2)], axis=1)
+
+                z = jnp.dot(wside[side], operand(load), preferred_element_type=F32)
+                w = fw_v[side, at, :]
+                for u in range(V):
+                    for j in range(2):
+                        image = z[u * 8 : u * 8 + 8, j * NR : (j + 1) * NR]
+                        rhs_v[u, k0 + j, at, :] = rhs_v[u, k0 + j, at, :] - w * image
+
     def main(c):
         k0 = 2 * c
 
-        def rows(x, t):
-            return pl.ds(x * CG + 8 * t, 8)
-
-        def pair(ref, *at):
-            return jnp.concatenate([ref[at[0], k0 + j, *at[1:]] for j in range(2)], axis=1)
-
-        def finish(x, left, image):
+        def finish(x, left):
             for t in range(2):
-                w = fw_v[1, rows(x, t), :]
-                rem = [
-                    [left[t][j][u] - w * image[t][u * 8 : u * 8 + 8, j * NR : (j + 1) * NR] for u in range(V)]
-                    for j in range(2)
-                ]
-                for u in range(V):
+                for j in range(2):
+                    acc = None
+                    for v in range(V):
+                        rhs_v[v, k0 + j, rows(x, t), :] = left[t][j][v]
+                        term = binv_v[0, v, rows(x, t), :] * left[t][j][v]
+                        acc = term if acc is None else acc + term
+                    upd[0, k0 + j, rows(x, t), :] = acc
+
+        before, left_before = None, None
+        for x in range(CX):
+            y = [
+                jnp.dot(
+                    wmain[...],
+                    operand(
+                        lambda v, t=t: jnp.concatenate(
+                            [it_v[v, k0 + j, rows(x, t), :] for j in range(2)], axis=1
+                        )
+                    ),
+                    preferred_element_type=F32,
+                )
+                for t in range(2)
+            ]
+
+            def part(t, f, u, j):
+                at = (u * 6 + f) * 8
+                return y[t][at : at + 8, j * NR : (j + 1) * NR]
+
+            w = [[fw_v[f, rows(x, t), :] for f in range(6)] for t in range(2)]
+            w[0][2] = jnp.where(sub == 0, 0.0, w[0][2])
+            w[1][3] = jnp.where(sub == 7, 0.0, w[1][3])
+            for t in range(2):
+                w[t][4] = jnp.where(lane == 0, 0.0, w[t][4])
+                w[t][5] = jnp.where(lane == NR - 1, 0.0, w[t][5])
+            left = [[[None] * V for _ in range(2)] for _ in range(2)]
+            kept = [[[None] * V for _ in range(2)] for _ in range(2)]
+            for u in range(V):
+                for t in range(2):
+                    for j in range(2):
+                        y2, y3 = part(t, 2, u, j), part(t, 3, u, j)
+                        if t == 1:
+                            y2 = jnp.where(sub == 0, part(0, 2, u, j), y2)
+                        else:
+                            y3 = jnp.where(sub == 7, part(1, 3, u, j), y3)
+                        total = w[t][2] * y2 + w[t][3] * y3
+                        total += w[t][4] * pltpu.roll(part(t, 4, u, j), 1, axis=1)
+                        total += w[t][5] * pltpu.roll(part(t, 5, u, j), NR - 1, axis=1)
+                        if x > 0:
+                            total += w[t][0] * before[t][j][u]
+                            left_before[t][j][u] = left_before[t][j][u] - fw_v[1, rows(x - 1, t), :] * part(t, 1, u, j)
+                        left[t][j][u] = rhs_v[u, k0 + j, rows(x, t), :] - total
+                        kept[t][j][u] = part(t, 0, u, j)
+            if x > 0:
+                finish(x - 1, left_before)
+            before, left_before = kept, left
+        finish(CX - 1, left_before)
+
+    def rest(first, last):
+        @pl.loop(first, last)
+        def _(i):
+            k0, x = 2 * (i // CX), i % CX
+            for t in range(2):
+                at = pl.ds(pl.multiple_of(x * CG + 8 * t, 8), 8)
+                rem = [[rhs_v[v, k0 + j, at, :] for v in range(V)] for j in range(2)]
+                for u in range(1, V):
                     acc = [None, None]
                     for v in range(V):
-                        b = binv_v[u, v, rows(x, t), :]
+                        b = binv_v[u, v, at, :]
                         for j in range(2):
                             term = b * rem[j][v]
                             acc[j] = term if acc[j] is None else acc[j] + term
                     for j in range(2):
-                        upd[u, k0 + j, rows(x, t), :] = acc[j]
-
-        def outer(side, t):
-            return jnp.dot(
-                wside[side],
-                operand(lambda v: pair(halo_x.at[side], v, pl.ds(8 * t, 8))),
-                preferred_element_type=F32,
-            )
-
-        for side in range(2):
-            edge[side] = jnp.dot(
-                wside[2 + side],
-                operand(lambda v: pair(halo_g.at[side], v)),
-                preferred_element_type=F32,
-            )
-        before, left_before = [outer(WEST, t) for t in range(2)], None
-        for x in range(CX):
-            y = [
-                jnp.dot(
-                    wmain[...],
-                    operand(lambda v, t=t: pair(it_v, v, rows(x, t))),
-                    preferred_element_type=F32,
-                )
-                for t in range(2)
-            ]
-
-            def part(t, f, u, j):
-                at = f * BLK + u * 8
-                return y[t][at : at + 8, j * NR : (j + 1) * NR]
-
-            w = [[fw_v[f, rows(x, t), :] for f in range(6)] for t in range(2)]
-            for t in range(2):
-                w[t][4] = jnp.where(lane == 0, 0.0, w[t][4])
-                w[t][5] = jnp.where(lane == NR - 1, 0.0, w[t][5])
-            left = [[[None] * V for _ in range(2)] for _ in range(2)]
-            for t in range(2):
-                for j in range(2):
-                    for u in range(V):
-                        at = u * 8 + x
-                        if t == 0:
-                            first = edge[0, at : at + 1, j * NR : (j + 1) * NR]
-                            last = part(1, 3, u, j)
-                        else:
-                            first = part(0, 2, u, j)
-                            last = edge[1, at : at + 1, j * NR : (j + 1) * NR]
-                        y2 = jnp.where(sub == 0, first, part(t, 2, u, j))
-                        y3 = jnp.where(sub == 7, last, part(t, 3, u, j))
-                        total = w[t][2] * y2 + w[t][3] * y3
-                        total += w[t][4] * pltpu.roll(part(t, 4, u, j), 1, axis=1)
-                        total += w[t][5] * pltpu.roll(part(t, 5, u, j), NR - 1, axis=1)
-                        total += w[t][0] * before[t][u * 8 : u * 8 + 8, j * NR : (j + 1) * NR]
-                        left[t][j][u] = rhs_v[u, k0 + j, rows(x, t), :] - total
-            if x > 0:
-                finish(x - 1, left_before, [y[t][BLK : 2 * BLK] for t in range(2)])
-            before, left_before = [y[t][0:BLK] for t in range(2)], left
-        finish(CX - 1, left_before, [outer(EAST, t) for t in range(2)])
+                        upd[u, k0 + j, at, :] = acc[j]
 
     r = lax.broadcasted_iota(jnp.int32, (2 * NR, SLOTS), 0)
     lanes = (cell[...] % NR == r % NR).astype(BF16)
@@ -301,6 +339,16 @@
             def _():
                 halo_copy(side, c, side).wait_recv()
 
+        for at, done, then in ((1, ((0, 0), (1, 0)), ((0, 1), (1, 1))), (3, ((0, 1), (1, 1)), ((1, 2),)), (5, ((1, 2),), ())):
+
+            @pl.when(c == at)
+            def _():
+                for axis, level in done:
+                    relay_wait(axis, level)
+                for axis, level in then:
+                    relay_signal(axis, level)
+
+        borders(c)
         main(c)
         for j in range(2):
             hi, lo = split(upd[0, 2 * c + j])
@@ -328,6 +376,7 @@
     for step in range(1, NS):
         stream_copy(step, s).start()
     arrived_1[pl.ds(pl.multiple_of(s * PACK_1, 8), PACK_1), :] = send_1[s]
+    rest(0, REST_1)
     for step in range(1, NS):
         stream_copy(step, lax.rem(s + NS - step, NS)).wait_recv()
     for to in range(NG):
@@ -340,6 +389,7 @@
     for step in range(1, NG):
         girth_copy(step, g).start()
     arrived_2[g] = send_2[g]
+    rest(REST_1, PAIRS * CX)
     for step in range(1, NG):
         girth_copy(step, lax.rem(g + NG - step, NG)).wait_recv()
     arrived_out[...] = arrived_2[...]
@@ -436,8 +486,7 @@
             pltpu.VMEM((2, V, K, CX, NR), F32),
             pltpu.VMEM((2, V, K, CX, NR), F32),
             pltpu.VMEM((6 * BLK, DEPTH), BF16),
-            pltpu.VMEM((4, 64, DEPTH), BF16),
-            pltpu.VMEM((2, 64, 2 * NR), F32),
+            pltpu.VMEM((4, TERM, DEPTH), BF16),
             pltpu.VMEM((K, SLOTS), F32),
             pltpu.VMEM((6, V, V), F32),
             pltpu.VMEM((1, SLOTS), jnp.int32),
@@ -457,6 +506,7 @@
             dma((NS,)),
             dma((NG,)),
             dma((NG,)),
+            pltpu.SemaphoreType.REGULAR((2, 3, 2)),
         ],
         compiler_params=pltpu.CompilerParams(
             collective_id=0, has_side_effects=True, vmem_limit_bytes=32 * 1024 * 1024

time: 44.3 us -> 39.8 us (0.90)
  Pallas kernels: 43.4 us -> 38.9 us
    pallas_call x1, Pallas kernels: 40.3 us -> 35.8 us  [shards(): pl.pallas_call(sweep_kernel, out_shape=(pltpu.VMEM((V, K, ROWS, NR), F32)...]
where the time goes in v2:
time: 39.8 us; the launch traced here: 39.5 us
  Pallas kernels  38.9 us (98%)
  between operations  0.64 us (2%)
    pallas_call x1, Pallas kernels, shards(): pl.pallas_call(sweep_kernel, out_shape=(pltpu.VMEM((V, K, ROWS, NR), F32)...  35.8 us
    pallas_call x1, Pallas kernels, shards(): pl.pallas_call(force_kernel, out_shape=(pltpu.HBM((V, K, ROWS, NR), F32),...  3.07 us

profile of v2, /device:TPU:1, one launch (start us, length us, event | category | flops | bytes accessed | tf_op | source)
XLA Modules:
  0.0 39.5 jit_solution(13449839305440764600)
XLA Ops:
  0.6 35.8 %shard_map.112 = (f32[7,16,128,128]{3,2,1,0:T(8,128)S(1)}, f32[16,24,128]{2,1,0:T(8,128)S(1)}) custom-call(f32[7,16,128,128]{3,2,1,0:T(8,128)} %bitcast.9, f32[7,16,128,128]{3,2,1,0:T(8,128)} %bitcast.10, f32[7,7,128,128]{3,2,1,0:T(8,128)} %bitcast.11, f32[6,128,128]{2,1,0:T(8,128)} %bitcast.12, f32[6,7,7]{2,1,0:T(8,128)} %jac_in.1, s32[1,256]{1,0:T(1,128)} %bitcast.14, ...), custom_call_target="tpu_custom_call" | custom-call | tf_op jit(solution)/shard_map/pallas_call | solution.py:472
  36.5 3.1 %shard_map.113 = (f32[7,16,128,128]{3,2,1,0:T(8,128)}, f32[32,128]{1,0:T(8,128)}, f32[8,16]{1,0:T(8,128)}) custom-call(f32[7,16,128,128]{3,2,1,0:T(8,128)S(1)} %get-tuple-element.8.upd, f32[16,24,128]{2,1,0:T(8,128)S(1)} %get-tuple-element.9.arrived), custom_call_target="tpu_custom_call" | custom-call | tf_op jit(solution)/shard_map/pallas_call | solution.py:515

commit v3 on v2

--- a/solution.py
+++ b/solution.py
@@ -17,8 +17,8 @@
 NG = 16
 DEV = NS * NG
 PAIRS = K // 2
-PACK_1 = 2 * NG + 8
-REST_1 = 32
+AHEAD = 3
+HEARD = (1, 4)
 BLK = V * 8
 TERM = 64
 DEPTH = 3 * TERM
@@ -27,6 +27,19 @@
 F32 = jnp.float32
 BF16 = jnp.bfloat16
 WEST, EAST, SOUTH, NORTH = range(4)
+STEPS = sorted(
+    [(a, b, c, d) for a in range(4) for b in range(2) for c in range(4) for d in range(4)][1:],
+    key=lambda o: -sum(min(n, 4 - n) for n in (o[0], o[2], o[3])),
+)
+NEAR = [(0, 1, 0, 0)] + [
+    (n if a == 0 else 0, b, n if a == 1 else 0, n if a == 2 else 0)
+    for a in range(3) for n in (1, 3) for b in range(2)
+]
+ROUNDS = (
+    tuple(o for o in NEAR if o[1] == 0),
+    tuple((n, 0, 0, 0) for n in (1, 2, 3)),
+    tuple((0, 0, n, 0) for n in (1, 2, 3)),
+)
 
 
 def nt(a, b, precision=None):
@@ -67,8 +80,8 @@
     it, rhs, binv, fw, jac_in, cell_in, owner_in, patch_in, shape_in,
     upd, arrived_out,
     it_v, rhs_v, binv_v, fw_v, halo_x, halo_g, send_g, wmain, wside, pick,
-    jac, cell, owner, patch, shape, send_1, arrived_1, send_2, arrived_2,
-    sem_it, sem_rhs, sem_misc, send_sem, recv_sem, send_sem_1, recv_sem_1, send_sem_2, recv_sem_2, relay,
+    jac, cell, owner, patch, shape, payload, arrived,
+    sem_it, sem_rhs, sem_misc, send_sem, recv_sem, out_sem, in_sem, relay,
 ):
     s, g = lax.axis_index("stream"), lax.axis_index("girth")
     present = (s > 0, s < NS - 1, g > 0, g < NG - 1)
@@ -114,58 +127,74 @@
             device_id_type=MESH,
         )
 
-    def stream_copy(step, land):
-        to = lax.rem(s + step, NS)
+    me = s * NG + g
+    y, core, z, x4 = s // 2, lax.rem(s, 2), g // 4, lax.rem(g, 4)
+    by_y = [2 * lax.rem(y + n, 4) for n in range(4)]
+    by_core = [lax.rem(core + n, 2) for n in range(2)]
+    by_z = [4 * lax.rem(z + n, 4) for n in range(4)]
+    by_x = [lax.rem(x4 + n, 4) for n in range(4)]
+
+    def at(step):
+        return (by_y[step[0]] + by_core[step[1]], by_z[step[2]] + by_x[step[3]])
+
+    def wall_copy(step):
+        to = at(step)
         return pltpu.make_async_remote_copy(
-            src_ref=send_1.at[to],
-            dst_ref=arrived_1.at[pl.ds(land * PACK_1, PACK_1)],
-            send_sem=send_sem_1.at[step],
-            recv_sem=recv_sem_1.at[land],
-            device_id=(to, g),
+            src_ref=payload.at[to[0] * NG + to[1]],
+            dst_ref=arrived.at[me],
+            send_sem=out_sem,
+            recv_sem=in_sem,
+            device_id=to,
             device_id_type=MESH,
         )
 
-    def girth_copy(step, land):
-        to = lax.rem(g + step, NG)
-        return pltpu.make_async_remote_copy(
-            src_ref=send_2.at[to],
-            dst_ref=arrived_2.at[land],
-            send_sem=send_sem_2.at[step],
-            recv_sem=recv_sem_2.at[land],
-            device_id=(s, to),
-            device_id_type=MESH,
-        )
-
-    def ring(axis, step):
-        if axis == 0:
-            return (lax.rem(s + step + NS, NS), g)
-        return (s, lax.rem(g + step + NG, NG))
-
-    def relay_signal(axis, level):
-        for way in range(2):
-            pl.semaphore_signal(
-                relay.at[axis, level, way],
-                inc=1,
-                device_id=ring(axis, (1 << level) * (1 - 2 * way)),
-                device_id_type=MESH,
-            )
-
-    def relay_wait(axis, level):
-        for way in range(2):
-            pl.semaphore_wait(relay.at[axis, level, way], 1)
-
-    barrier = pltpu.get_barrier_semaphore()
-    for axis in range(2):
-        for step in (1, -1):
-            pl.semaphore_signal(barrier, inc=1, device_id=ring(axis, step), device_id_type=MESH)
-
-    for copy in singles[:5]:
-        copy.start()
+    others = pl.ds(0, DEV - 1)
+    wall_all = pltpu.make_async_remote_copy(
+        src_ref=payload.at[others],
+        dst_ref=arrived.at[others],
+        send_sem=out_sem,
+        recv_sem=in_sem,
+        device_id=(by_y[0] + by_core[1], g),
+        device_id_type=MESH,
+    )
+
+    def relay_signal(level):
+        for i, step in enumerate(ROUNDS[level]):
+            pl.semaphore_signal(relay.at[level, i], inc=1, device_id=at(step), device_id_type=MESH)
+
+    def relay_wait(level):
+        for i in range(len(ROUNDS[level])):
+            pl.semaphore_wait(relay.at[level, i], 1)
+
     for c in range(PAIRS):
         it_copy(c).start()
-    for copy in singles[5:]:
+
+    barrier = pltpu.get_barrier_semaphore()
+    for to in [at(step) for step in NEAR] + [(s, lax.rem(g + 1, NG)), (s, lax.rem(g + NG - 1, NG))]:
+        pl.semaphore_signal(barrier, inc=1, device_id=to, device_id_type=MESH)
+
+    for copy in singles:
         copy.start()
+    for c in range(AHEAD):
+        rhs_copy(c).start()
+
     for c in range(PAIRS):
+        it_copy(c).wait()
+        for k in (2 * c, 2 * c + 1):
+            for v in range(V):
+                send_g[0, v, k] = it_v[v, k, pl.ds(0, CX, stride=CG), :]
+                send_g[1, v, k] = it_v[v, k, pl.ds(CG - 1, CX, stride=CG), :]
+        if c == 3:
+            pl.semaphore_wait(barrier, len(NEAR) + 2)
+        for d in range(4) if c == 3 else ([c] if c > 3 else []):
+            for side in range(4):
+
+                @pl.when(present[side])
+                def _():
+                    halo_copy(side, d).start()
+
+    relay_signal(0)
+    for c in range(AHEAD, PAIRS):
         rhs_copy(c).start()
 
     for side in range(4):
@@ -188,25 +217,6 @@
     pad = jnp.zeros((TERM - BLK, DEPTH), F32)
     for f in range(4):
         wside[f] = jnp.concatenate([operator(jac[f], 0), pad], axis=0).astype(BF16)
-
-    for c in range(PAIRS):
-        it_copy(c).wait()
-        for k in (2 * c, 2 * c + 1):
-            for v in range(V):
-                send_g[0, v, k] = it_v[v, k, pl.ds(0, CX, stride=CG), :]
-                send_g[1, v, k] = it_v[v, k, pl.ds(CG - 1, CX, stride=CG), :]
-
-    pl.semaphore_wait(barrier, 4)
-
-    for c in range(PAIRS):
-        for side in range(4):
-
-            @pl.when(present[side])
-            def _():
-                halo_copy(side, c).start()
-
-    relay_signal(0, 0)
-    relay_signal(1, 0)
 
     names = (owner[...] == lax.broadcasted_iota(jnp.int32, (DEV, SLOTS), 0)).astype(F32)
     r = lax.broadcasted_iota(jnp.int32, (SLOTS, SLOTS), 0)
@@ -339,14 +349,12 @@
             def _():
                 halo_copy(side, c, side).wait_recv()
 
-        for at, done, then in ((1, ((0, 0), (1, 0)), ((0, 1), (1, 1))), (3, ((0, 1), (1, 1)), ((1, 2),)), (5, ((1, 2),), ())):
-
-            @pl.when(c == at)
+        for level, when in enumerate(HEARD):
+
+            @pl.when(c == when)
             def _():
-                for axis, level in done:
-                    relay_wait(axis, level)
-                for axis, level in then:
-                    relay_signal(axis, level)
+                relay_wait(level)
+                relay_signal(level + 1)
 
         borders(c)
         main(c)
@@ -367,32 +375,18 @@
     chosen = jnp.concatenate([chosen, chosen], axis=1)
     for half in range(2):
         hi, lo = split(jnp.where(place == 4 * half + group, spread, 0.0))
-        packed = nt(chosen, jnp.concatenate([hi, lo], axis=1).astype(BF16))
-        send_1[:, NG * half : NG * (half + 1), :] = packed.reshape(NS, NG, NR)
+        payload[:, half, :] = nt(chosen, jnp.concatenate([hi, lo], axis=1).astype(BF16))
     products = jnp.concatenate([shapes[m : m + 1] * pressure for m in range(8)], axis=0)
     sums = nt(jnp.ones((8, SLOTS), F32), products, HIGH)
-    send_1[:, 2 * NG :, :] = jnp.broadcast_to(sums[None], (NS, 8, NR))
-
-    for step in range(1, NS):
-        stream_copy(step, s).start()
-    arrived_1[pl.ds(pl.multiple_of(s * PACK_1, 8), PACK_1), :] = send_1[s]
-    rest(0, REST_1)
-    for step in range(1, NS):
-        stream_copy(step, lax.rem(s + NS - step, NS)).wait_recv()
-    for to in range(NG):
-        for half in range(2):
-            send_2[to, 8 * half : 8 * half + 8, :] = arrived_1[
-                pl.ds(half * NG + to, NS, stride=PACK_1), :
-            ]
-    sums = jnp.sum(arrived_1[pl.ds(2 * NG, NS, stride=PACK_1), :], axis=0, keepdims=True)
-    send_2[:, 16:, :] = jnp.broadcast_to(sums[None], (NG, 8, NR))
-    for step in range(1, NG):
-        girth_copy(step, g).start()
-    arrived_2[g] = send_2[g]
-    rest(REST_1, PAIRS * CX)
-    for step in range(1, NG):
-        girth_copy(step, lax.rem(g + NG - step, NG)).wait_recv()
-    arrived_out[...] = arrived_2[...]
+    payload[:, 2, :] = jnp.broadcast_to(sums[0:1], (DEV, NR))
+
+    relay_wait(len(ROUNDS) - 1)
+    for step in STEPS:
+        wall_copy(step).start()
+    arrived[me] = payload[me]
+    rest(0, PAIRS * CX)
+    wall_all.wait_recv()
+    arrived_out[...] = arrived[...]
 
     for c in range(PAIRS):
         for side in range(4):
@@ -401,10 +395,7 @@
             def _():
                 halo_copy(side, c).wait_send()
 
-    for step in range(1, NS):
-        stream_copy(step, s).wait_send()
-    for step in range(1, NG):
-        girth_copy(step, g).wait_send()
+    wall_all.wait_send()
 
 
 def force_kernel(upd, arrived, upd_out, patch_out, force_out, patch_force, force, sem):
@@ -419,7 +410,7 @@
     patch = lax.broadcasted_iota(jnp.int32, (DEV, NR), 1).astype(F32)
     total = None
     for half in range(2):
-        hi, lo = split(arrived[:, 8 * half : 8 * half + 8, :].reshape(DEV, NR))
+        hi, lo = split(arrived[:, half, :])
         both = jnp.concatenate([hi, lo], axis=1).astype(BF16)
         for j in range(4):
             base = 32 * j
@@ -439,7 +430,7 @@
     patch_force[...] = total
     out_patch = pltpu.make_async_copy(patch_force, patch_out, sem.at[V])
     out_patch.start()
-    sums = jnp.sum(arrived[:, 16, :], axis=0, keepdims=True) / jnp.sqrt(F32(DEV * SLOTS))
+    sums = jnp.sum(arrived[:, 2, :], axis=0, keepdims=True) / jnp.sqrt(F32(DEV * SLOTS))
     r = lax.broadcasted_iota(jnp.int32, (8, NR), 0)
     c = lax.broadcasted_iota(jnp.int32, (8, NR), 1)
     rows = jnp.where(c // K == r, sums, 0.0)
@@ -473,7 +464,7 @@
         sweep_kernel,
         out_shape=(
             pltpu.VMEM((V, K, ROWS, NR), F32),
-            pltpu.VMEM((NG, 24, NR), F32),
+            pltpu.VMEM((DEV, 3, NR), F32),
         ),
         in_specs=[hbm] * 9,
         out_specs=(vmem, vmem),
@@ -493,20 +484,16 @@
             pltpu.VMEM((1, SLOTS), jnp.int32),
             pltpu.VMEM((1, SLOTS), jnp.int32),
             pltpu.VMEM((8, SLOTS), F32),
-            pltpu.VMEM((NS, PACK_1, NR), F32),
-            pltpu.VMEM((NS * PACK_1, NR), F32),
-            pltpu.VMEM((NG, 24, NR), F32),
-            pltpu.VMEM((NG, 24, NR), F32),
+            pltpu.VMEM((DEV, 3, NR), F32),
+            pltpu.VMEM((DEV, 3, NR), F32),
             dma((PAIRS,)),
             dma((PAIRS,)),
             dma((7,)),
             dma((4, PAIRS)),
             dma((4, PAIRS)),
-            dma((NS,)),
-            dma((NS,)),
-            dma((NG,)),
-            dma((NG,)),
-            pltpu.SemaphoreType.REGULAR((2, 3, 2)),
+            dma,
+            dma,
+            pltpu.SemaphoreType.REGULAR((3, 6)),
         ],
         compiler_params=pltpu.CompilerParams(
             collective_id=0, has_side_effects=True, vmem_limit_bytes=32 * 1024 * 1024

time: 39.8 us -> 34.1 us (0.86)
  Pallas kernels: 38.9 us -> 33.3 us
    pallas_call x1, Pallas kernels: 35.8 us -> 30.3 us  [shards(): pl.pallas_call(sweep_kernel, out_shape=(pltpu.VMEM((V, K, ROWS, NR), F32)...]
where the time goes in v3:
time: 34.1 us; the launch traced here: 34 us
  Pallas kernels  33.3 us (98%)
  between operations  0.64 us (2%)
    pallas_call x1, Pallas kernels, shards(): pl.pallas_call(sweep_kernel, out_shape=(pltpu.VMEM((V, K, ROWS, NR), F32)...  30.3 us
    pallas_call x1, Pallas kernels, shards(): pl.pallas_call(force_kernel, out_shape=(pltpu.HBM((V, K, ROWS, NR), F32),...  3.07 us

profile of v3, /device:TPU:1, one launch (start us, length us, event | category | flops | bytes accessed | tf_op | source)
XLA Modules:
  0.0 34.0 jit_solution(5385505633774082378)
XLA Ops:
  0.6 30.3 %shard_map.112 = (f32[7,16,128,128]{3,2,1,0:T(8,128)S(1)}, f32[128,3,128]{2,1,0:T(4,128)S(1)}) custom-call(f32[7,16,128,128]{3,2,1,0:T(8,128)} %bitcast.9, f32[7,16,128,128]{3,2,1,0:T(8,128)} %bitcast.10, f32[7,7,128,128]{3,2,1,0:T(8,128)} %bitcast.11, f32[6,128,128]{2,1,0:T(8,128)} %bitcast.12, f32[6,7,7]{2,1,0:T(8,128)} %jac_in.1, s32[1,256]{1,0:T(1,128)} %bitcast.14, ...), custom_call_target="tpu_custom_call" | custom-call | tf_op jit(solution)/shard_map/pallas_call | solution.py:463
  30.9 3.1 %shard_map.113 = (f32[7,16,128,128]{3,2,1,0:T(8,128)}, f32[32,128]{1,0:T(8,128)}, f32[8,16]{1,0:T(8,128)}) custom-call(f32[7,16,128,128]{3,2,1,0:T(8,128)S(1)} %get-tuple-element.8.upd, f32[128,3,128]{2,1,0:T(4,128)S(1)} %get-tuple-element.9.arrived), custom_call_target="tpu_custom_call" | custom-call | tf_op jit(solution)/shard_map/pallas_call | solution.py:502

commit v4 on v3

--- a/solution.py
+++ b/solution.py
@@ -17,7 +17,6 @@
 NG = 16
 DEV = NS * NG
 PAIRS = K // 2
-AHEAD = 3
 HEARD = (1, 4)
 BLK = V * 8
 TERM = 64
@@ -166,36 +165,37 @@
         for i in range(len(ROUNDS[level])):
             pl.semaphore_wait(relay.at[level, i], 1)
 
-    for c in range(PAIRS):
-        it_copy(c).start()
-
-    barrier = pltpu.get_barrier_semaphore()
-    for to in [at(step) for step in NEAR] + [(s, lax.rem(g + 1, NG)), (s, lax.rem(g + NG - 1, NG))]:
-        pl.semaphore_signal(barrier, inc=1, device_id=to, device_id_type=MESH)
-
-    for copy in singles:
-        copy.start()
-    for c in range(AHEAD):
-        rhs_copy(c).start()
-
-    for c in range(PAIRS):
+    def send(c):
         it_copy(c).wait()
         for k in (2 * c, 2 * c + 1):
             for v in range(V):
                 send_g[0, v, k] = it_v[v, k, pl.ds(0, CX, stride=CG), :]
                 send_g[1, v, k] = it_v[v, k, pl.ds(CG - 1, CX, stride=CG), :]
-        if c == 3:
-            pl.semaphore_wait(barrier, len(NEAR) + 2)
-        for d in range(4) if c == 3 else ([c] if c > 3 else []):
-            for side in range(4):
-
-                @pl.when(present[side])
-                def _():
-                    halo_copy(side, d).start()
-
+        for side in range(4):
+
+            @pl.when(present[side])
+            def _():
+                halo_copy(side, c).start()
+
+    for c in range(2):
+        it_copy(c).start()
+
+    barrier = pltpu.get_barrier_semaphore()
+    for to in [at(step) for step in NEAR] + [(s, lax.rem(g + 1, NG)), (s, lax.rem(g + NG - 1, NG))]:
+        pl.semaphore_signal(barrier, inc=1, device_id=to, device_id_type=MESH)
+
+    for copy in singles:
+        copy.start()
+    rhs_copy(0).start()
+
+    pl.semaphore_wait(barrier, len(NEAR) + 2)
+    for c in range(2):
+        send(c)
+    for c in range(2, PAIRS):
+        it_copy(c).start()
+    for c in range(1, PAIRS):
+        rhs_copy(c).start()
     relay_signal(0)
-    for c in range(AHEAD, PAIRS):
-        rhs_copy(c).start()
 
     for side in range(4):
 
@@ -238,24 +238,28 @@
         for side in range(4):
             for t in range(2 if side in (WEST, EAST) else 1):
                 if side in (WEST, EAST):
-                    at = rows(0 if side == WEST else CX - 1, t)
+                    where = rows(0 if side == WEST else CX - 1, t)
 
                     def load(v):
                         return jnp.concatenate(
                             [halo_x[side, v, k0 + j, pl.ds(8 * t, 8), :] for j in range(2)], axis=1
                         )
                 else:
-                    at = pl.ds(0 if side == SOUTH else CG - 1, CX, stride=CG)
+                    where = pl.ds(0 if side == SOUTH else CG - 1, CX, stride=CG)
 
                     def load(v):
                         return jnp.concatenate([halo_g[side - 2, v, k0 + j] for j in range(2)], axis=1)
 
                 z = jnp.dot(wside[side], operand(load), preferred_element_type=F32)
-                w = fw_v[side, at, :]
-                for u in range(V):
-                    for j in range(2):
-                        image = z[u * 8 : u * 8 + 8, j * NR : (j + 1) * NR]
-                        rhs_v[u, k0 + j, at, :] = rhs_v[u, k0 + j, at, :] - w * image
+                w = fw_v[side, where, :]
+                for j in range(2):
+                    change = None
+                    for u in range(V):
+                        image = w * z[u * 8 : u * 8 + 8, j * NR : (j + 1) * NR]
+                        rhs_v[u, k0 + j, where, :] = rhs_v[u, k0 + j, where, :] - image
+                        term = binv_v[0, u, where, :] * image
+                        change = term if change is None else change + term
+                    upd[0, k0 + j, where, :] = upd[0, k0 + j, where, :] - change
 
     def main(c):
         k0 = 2 * c
@@ -340,29 +344,40 @@
     r = lax.broadcasted_iota(jnp.int32, (ROWS, SLOTS), 0)
     on_row = (cell[...] // NR == r).astype(F32)
 
-    @pl.loop(0, PAIRS)
-    def _(c):
-        rhs_copy(c).wait()
-        for side in range(4):
-
-            @pl.when(present[side])
-            def _():
-                halo_copy(side, c, side).wait_recv()
-
+    @pl.loop(0, PAIRS + 1)
+    def _(i):
         for level, when in enumerate(HEARD):
 
-            @pl.when(c == when)
+            @pl.when(i == when)
             def _():
                 relay_wait(level)
                 relay_signal(level + 1)
 
-        borders(c)
-        main(c)
-        for j in range(2):
-            hi, lo = split(upd[0, 2 * c + j])
-            both = jnp.concatenate([hi, lo], axis=1).astype(BF16)
-            found = jnp.dot(both, lanes, preferred_element_type=F32) * on_row
-            pick[pl.ds(2 * c + j, 1), :] = jnp.sum(found, axis=0, keepdims=True)
+        @pl.when(i < PAIRS // 2 - 1)
+        def _():
+            send(2 * i + 2)
+            send(2 * i + 3)
+
+        @pl.when(i < PAIRS)
+        def _():
+            rhs_copy(i).wait()
+            main(i)
+
+        @pl.when(i > 0)
+        def _():
+            c = i - 1
+            for side in range(4):
+
+                @pl.when(present[side])
+                def _():
+                    halo_copy(side, c, side).wait_recv()
+
+            borders(c)
+            for j in range(2):
+                hi, lo = split(upd[0, 2 * c + j])
+                both = jnp.concatenate([hi, lo], axis=1).astype(BF16)
+                found = jnp.dot(both, lanes, preferred_element_type=F32) * on_row
+                pick[pl.ds(2 * c + j, 1), :] = jnp.sum(found, axis=0, keepdims=True)
 
     pressure = pick[...]
     shapes = shape[...]
@@ -385,9 +400,6 @@
         wall_copy(step).start()
     arrived[me] = payload[me]
     rest(0, PAIRS * CX)
-    wall_all.wait_recv()
-    arrived_out[...] = arrived[...]
-
     for c in range(PAIRS):
         for side in range(4):
 
@@ -395,15 +407,15 @@
             def _():
                 halo_copy(side, c).wait_send()
 
+    wall_all.wait_recv()
+    arrived_out[...] = arrived[...]
+
     wall_all.wait_send()
 
 
 def force_kernel(upd, arrived, upd_out, patch_out, force_out, patch_force, force, sem):
-    copies = [
-        pltpu.make_async_copy(upd.at[v], upd_out.at[v], sem.at[v]) for v in range(V)
-    ]
-    for copy in copies:
-        copy.start()
+    out_field = pltpu.make_async_copy(upd, upd_out, sem.at[2])
+    out_field.start()
 
     lane = lax.broadcasted_iota(jnp.int32, (2 * NR, NR), 0) % NR
     column = lax.broadcasted_iota(jnp.int32, (2 * NR, NR), 1)
@@ -428,7 +440,7 @@
             )
             total = term if total is None else total + term
     patch_force[...] = total
-    out_patch = pltpu.make_async_copy(patch_force, patch_out, sem.at[V])
+    out_patch = pltpu.make_async_copy(patch_force, patch_out, sem.at[0])
     out_patch.start()
     sums = jnp.sum(arrived[:, 2, :], axis=0, keepdims=True) / jnp.sqrt(F32(DEV * SLOTS))
     r = lax.broadcasted_iota(jnp.int32, (8, NR), 0)
@@ -437,10 +449,9 @@
     r = lax.broadcasted_iota(jnp.int32, (K, NR), 0)
     c = lax.broadcasted_iota(jnp.int32, (K, NR), 1)
     force[...] = nt(rows, (c % K == r).astype(F32), HIGH)
-    out_force = pltpu.make_async_copy(force, force_out, sem.at[V + 1])
+    out_force = pltpu.make_async_copy(force, force_out, sem.at[1])
     out_force.start()
-    for copy in copies:
-        copy.wait()
+    out_field.wait()
     out_patch.wait()
     out_force.wait()
 
@@ -511,7 +522,7 @@
         scratch_shapes=[
             pltpu.VMEM((PATCH_DEV, NR), F32),
             pltpu.VMEM((8, K), F32),
-            dma((V + 2,)),
+            dma((3,)),
         ],
         compiler_params=pltpu.CompilerParams(vmem_limit_bytes=8 * 1024 * 1024),
     )(

time: 34.1 us -> 33.8 us (level)
  no operation moved by 1% of the time
where the time goes in v4:
time: 33.8 us; the launch traced here: 33.7 us
  Pallas kernels  33.1 us (98%)
  between operations  0.64 us (2%)
    pallas_call x1, Pallas kernels, shards(): pl.pallas_call(sweep_kernel, out_shape=(pltpu.VMEM((V, K, ROWS, NR), F32)...  30 us
    pallas_call x1, Pallas kernels, shards(): pl.pallas_call(force_kernel, out_shape=(pltpu.HBM((V, K, ROWS, NR), F32),...  3.08 us

profile of v4, /device:TPU:1, one launch (start us, length us, event | category | flops | bytes accessed | tf_op | source)
XLA Modules:
  0.0 33.7 jit_solution(15874736016428925819)
XLA Ops:
  0.6 30.0 %shard_map.112 = (f32[7,16,128,128]{3,2,1,0:T(8,128)S(1)}, f32[128,3,128]{2,1,0:T(4,128)S(1)}) custom-call(f32[7,16,128,128]{3,2,1,0:T(8,128)} %bitcast.9, f32[7,16,128,128]{3,2,1,0:T(8,128)} %bitcast.10, f32[7,7,128,128]{3,2,1,0:T(8,128)} %bitcast.11, f32[6,128,128]{2,1,0:T(8,128)} %bitcast.12, f32[6,7,7]{2,1,0:T(8,128)} %jac_in.1, s32[1,256]{1,0:T(1,128)} %bitcast.14, ...), custom_call_target="tpu_custom_call" | custom-call | tf_op jit(solution)/shard_map/pallas_call | solution.py:474
  30.6 3.1 %shard_map.113 = (f32[7,16,128,128]{3,2,1,0:T(8,128)}, f32[32,128]{1,0:T(8,128)}, f32[8,16]{1,0:T(8,128)}) custom-call(f32[7,16,128,128]{3,2,1,0:T(8,128)S(1)} %get-tuple-element.8.upd, f32[128,3,128]{2,1,0:T(4,128)S(1)} %get-tuple-element.9.arrived), custom_call_target="tpu_custom_call" | custom-call | tf_op jit(solution)/shard_map/pallas_call | solution.py:513
